TPU v7x, 32 devices: a whole 2x2x4 slice. The times are simulated.
32 devices in a mesh: member: 4 (over y, x), lat: 8 (over z, core).
Axes of the slice: x: 2, y: 2, z: 4, core: 2. Of those that a mesh axis runs over, the one named last changes fastest.
Arguments:
- state_now: float32 [8, 96, 180, 633], P('member', 'lat'), may hold values from -6 to 6
- sample_random_maps: float32 [8, 96, 180, 8], P('member', 'lat'), may hold values from -6 to 6
- noise_scale: float32 [8, 8], P('member'), may hold values from 0.2 to 2
- spec_gain: float32 [91, 641], replicated, may hold values from 0.2 to 1.8
- weight_in: float32 [641, 1282], replicated, may hold values from -0.25 to 0.25
- bias_in: float32 [1282], replicated, may hold values from -3 to 3
- weight_out: float32 [1282, 641], replicated, may hold values from -0.15625 to 0.15625
- bias_out: float32 [641], replicated, may hold values from -3 to 3
- targets: float32 [2, 96, 180, 633], P(None, 'lat'), may hold values from -6 to 6
- date_of: int32 [8], replicated, may hold values from 0 to 1, as said below
- row_slot: int32 [90], replicated, may hold values from 0 to 95, as said below
Outputs:
- crps_loss: float32 [], replicated
- layer_output: float32 [8, 96, 180, 641], P('member', 'lat')
- grad_state: float32 [8, 96, 180, 633], P('member', 'lat')
- grad_scale: float32 [8, 8], P('member')
- grad_gain: float32 [91, 641], replicated
- grad_weight_in: float32 [641, 1282], replicated
- grad_bias_in: float32 [1282], replicated
- grad_weight_out: float32 [1282, 641], replicated
- grad_bias_out: float32 [641], replicated
Inputs may be any that keep to these rules, and one draw needn't show every extreme that they name: `date_of`: each of the 2 dates is named by exactly 4 members. `row_slot`: strictly increasing, north to south; slot s lies on lat index s // 12; the first and the last lat index hold 12 rows each.
All inputs are finite; a program needn't handle non-finite values.
Results may differ from a plain program's by a relative error of at most 0.0003.
Values sent between devices are 32-bit elements; how exact they have to be, the bound alone decides.
A program may use at most 384 MiB of HBM per device.

v0:
```python
import math

import jax
import jax.numpy as jnp
from jax import lax
from jax.sharding import PartitionSpec as P

VARIABLE_COUNT = 633
LMAX = 90
NLAT = 90
NLON = 180
ENSEMBLE_SIZE = 4
DATES = 2


def legendre(colatitude, orders):
    cosine = jnp.cos(colatitude)[None, :]
    log_sine = jnp.log(jnp.sin(colatitude))[None, :]
    order_col = orders[:, None]
    log_start = (
        0.5
        * (
            jnp.log(2.0 * order_col + 1.0)
            - math.log(4.0 * math.pi)
            + lax.lgamma(order_col + 0.5)
            - 0.5 * math.log(math.pi)
            - lax.lgamma(order_col + 1.0)
        )
        + order_col * log_sine
    )
    start_value = jnp.exp(log_start)
    blank_rows = jnp.zeros((orders.shape[0], colatitude.shape[0]), jnp.float32)

    def degree_step(carry, degree):
        latest, earlier = carry
        degree_value = degree.astype(jnp.float32)
        previous = degree_value - 1.0
        factor = jnp.sqrt(
            (4.0 * degree_value * degree_value - 1.0)
            / jnp.maximum(degree_value * degree_value - order_col * order_col, 1.0)
        )
        shrink = jnp.sqrt(
            jnp.maximum(previous * previous - order_col * order_col, 0.0)
            / jnp.maximum(4.0 * previous * previous - 1.0, 1.0)
        )
        recursed = factor * (cosine * latest - shrink * earlier)
        newest = jnp.where(
            degree_value < order_col,
            0.0,
            jnp.where(degree_value == order_col, start_value, recursed),
        )
        return ((newest, latest), newest)

    _, stacked = lax.scan(
        degree_step, (blank_rows, blank_rows), jnp.arange(LMAX + 1, dtype=jnp.int32)
    )
    return jnp.transpose(stacked, (1, 0, 2))


def fourier_tables(lon_count, order_list):
    column = jnp.arange(lon_count, dtype=jnp.int32)[:, None]
    wave = order_list[None, :]
    phase = column * wave % lon_count
    angle = 2.0 * math.pi / lon_count * phase.astype(jnp.float32)
    keeping = (wave <= LMAX).astype(jnp.float32)
    basis = jnp.stack([jnp.cos(angle) * keeping, -jnp.sin(angle) * keeping], axis=-1)
    doubling = jnp.where((wave == 0) | (2 * wave == lon_count), 1.0, 2.0).astype(jnp.float32)
    return (basis * (2.0 * math.pi / lon_count), basis * doubling[:, :, None])


def slot_geometry(row_slot, first_slot, slot_total):
    lat_ids = jnp.arange(NLAT, dtype=jnp.int32)
    slot_ids = first_slot + jnp.arange(slot_total, dtype=jnp.int32)
    matches = (row_slot[:, None] == slot_ids[None, :]).astype(jnp.float32)
    used_slots = jnp.sum(matches, axis=0)
    lat_index = jnp.sum(matches * lat_ids[:, None].astype(jnp.float32), axis=0)
    colatitude = jnp.where(used_slots > 0.5, (lat_index + 0.5) * (math.pi / NLAT), 0.5 * math.pi)
    sine_rows = jnp.sin((lat_ids.astype(jnp.float32) + 0.5) * (math.pi / NLAT))
    quadrature = used_slots * (math.pi / NLAT) * jnp.sin(colatitude)
    area_weight = used_slots * NLAT * jnp.sin(colatitude) / jnp.sum(sine_rows)
    return (colatitude, used_slots, quadrature, area_weight)


def softened_modulus(value):
    return jnp.sqrt(value * value + 1.0)


def soft_sign(value):
    return value / jnp.sqrt(value * value + 1.0)


def gelu_slope(value):
    return 0.5 * (1.0 + lax.erf(value * (1.0 / math.sqrt(2.0)))) + value * jnp.exp(
        -0.5 * value * value
    ) * (1.0 / math.sqrt(2.0 * math.pi))


def local(
    state_now,
    sample_random_maps,
    noise_scale,
    spec_gain,
    weight_in,
    bias_in,
    weight_out,
    bias_out,
    targets,
    date_of,
    row_slot,
):
    highest = lax.Precision.HIGHEST
    samples_each_processor, rows_dev, lon_count, variable_dimension = state_now.shape
    lat_devices = lax.axis_size("lat")
    lat_rank = lax.axis_index("lat")
    member_rank = lax.axis_index("member")
    slot_count = rows_dev * lat_devices
    waves_dev = (LMAX + lat_devices) // lat_devices
    wave_count = waves_dev * lat_devices
    _, used_own, _, area_own = slot_geometry(row_slot, lat_rank * rows_dev, rows_dev)
    colat_all, _, quad_all, _ = slot_geometry(row_slot, 0, slot_count)
    slot_list = jnp.arange(wave_count, dtype=jnp.int32)
    wave_ids = lax.dynamic_slice_in_dim(slot_list, lat_rank * waves_dev, waves_dev, 0)
    legendre_table = (
        legendre(colat_all, wave_ids.astype(jnp.float32))
        * (wave_ids <= LMAX).astype(jnp.float32)[:, None, None]
    )
    weighted_table = legendre_table * quad_all[None, None, :]
    forward_table, inverse_table = fourier_tables(lon_count, slot_list)
    inputs = jnp.concatenate(
        [state_now, noise_scale[:, None, None, :] * sample_random_maps], axis=-1
    )
    width = inputs.shape[-1]
    spectral_rows = jnp.einsum("brkc,kmp->brmpc", inputs, forward_table, precision=highest)
    spectral_cols = lax.all_to_all(spectral_rows, "lat", split_axis=2, concat_axis=1, tiled=True)
    coeffs = jnp.einsum("dls,bsdpc->bldpc", weighted_table, spectral_cols, precision=highest)
    filtered = coeffs * spec_gain[None, :, None, None, :]
    synth_cols = jnp.einsum("dls,bldpc->bsdpc", legendre_table, filtered, precision=highest)
    synth_rows = lax.all_to_all(synth_cols, "lat", split_axis=1, concat_axis=2, tiled=True)
    smooth = jnp.einsum("brmpc,kmp->brkc", synth_rows, inverse_table, precision=highest)
    mixed_flat = (inputs + smooth).reshape(-1, width)
    hidden_pre = jnp.dot(mixed_flat, weight_in, precision=highest) + bias_in
    activated = jax.nn.gelu(hidden_pre, approximate=False)
    block_flat = mixed_flat + jnp.dot(activated, weight_out, precision=highest) + bias_out
    layer_output = block_flat.reshape(inputs.shape) * used_own[None, :, None, None]
    sample_prediction = layer_output[..., :variable_dimension]
    groups = jnp.argsort(date_of, stable=True).reshape(-1, ENSEMBLE_SIZE)
    pair_scale = 1.0 / (ENSEMBLE_SIZE * (ENSEMBLE_SIZE - 1))
    whole_ensemble_collected = lax.all_gather(sample_prediction, "member", axis=0, tiled=True)
    own_ids = member_rank * samples_each_processor + jnp.arange(
        samples_each_processor, dtype=jnp.int32
    )
    own_dates = jnp.take(date_of, own_ids, axis=0)
    mates = jnp.take(groups, own_dates, axis=0)
    companion_latitudes = jnp.take(whole_ensemble_collected, mates.reshape(-1), axis=0).reshape(
        (samples_each_processor, ENSEMBLE_SIZE) + sample_prediction.shape[1:]
    )
    observed_latitude_entries = jnp.take(targets, own_dates, axis=0)
    sample_deviation = sample_prediction - observed_latitude_entries
    sample_dispersion = sample_prediction[:, None] - companion_latitudes
    latitude_cosine_factors = area_own[None, :, None, None]
    partial_loss = jnp.sum(
        latitude_cosine_factors
        * (
            softened_modulus(sample_deviation) / ENSEMBLE_SIZE
            - 0.5 * pair_scale * (jnp.sum(softened_modulus(sample_dispersion), axis=1) - 1.0)
        )
    )
    prediction_cotangent = latitude_cosine_factors * (
        soft_sign(sample_deviation) / ENSEMBLE_SIZE
        - pair_scale * jnp.sum(soft_sign(sample_dispersion), axis=1)
    )
    grad_out = jnp.concatenate(
        [prediction_cotangent, jnp.zeros(sample_random_maps.shape, jnp.float32)], axis=-1
    ).reshape(-1, width)
    grad_bias_out_part = jnp.sum(grad_out, axis=0)
    grad_weight_out_part = jnp.einsum("th,tc->hc", activated, grad_out, precision=highest)
    grad_pre = jnp.einsum("tc,hc->th", grad_out, weight_out, precision=highest) * gelu_slope(
        hidden_pre
    )
    grad_bias_in_part = jnp.sum(grad_pre, axis=0)
    grad_weight_in_part = jnp.einsum("tc,th->ch", mixed_flat, grad_pre, precision=highest)
    grad_mixed = (
        grad_out + jnp.einsum("th,ch->tc", grad_pre, weight_in, precision=highest)
    ).reshape(inputs.shape)
    back_rows = jnp.einsum("brkc,kmp->brmpc", grad_mixed, inverse_table, precision=highest)
    back_cols = lax.all_to_all(back_rows, "lat", split_axis=2, concat_axis=1, tiled=True)
    back_coeffs = jnp.einsum("dls,bsdpc->bldpc", legendre_table, back_cols, precision=highest)
    grad_gain_part = jnp.einsum("bldpc,bldpc->lc", coeffs, back_coeffs, precision=highest)
    spread_cols = jnp.einsum(
        "dls,bldpc->bsdpc",
        weighted_table,
        back_coeffs * spec_gain[None, :, None, None, :],
        precision=highest,
    )
    spread_rows = lax.all_to_all(spread_cols, "lat", split_axis=1, concat_axis=2, tiled=True)
    grad_inputs = grad_mixed + jnp.einsum(
        "brmpc,kmp->brkc", spread_rows, forward_table, precision=highest
    )
    grad_state = grad_inputs[..., :variable_dimension] * used_own[None, :, None, None]
    scale_part = jnp.sum(grad_inputs[..., variable_dimension:] * sample_random_maps, axis=(1, 2))
    grad_scale = lax.psum(scale_part, "lat")
    grad_weight_in, grad_bias_in, grad_weight_out, grad_bias_out, grad_gain, total_sum = lax.psum(
        (
            grad_weight_in_part,
            grad_bias_in_part,
            grad_weight_out_part,
            grad_bias_out_part,
            grad_gain_part,
            partial_loss,
        ),
        ("member", "lat"),
    )
    crps_loss = total_sum / (DATES * NLAT * NLON * VARIABLE_COUNT)
    return (
        crps_loss,
        layer_output,
        grad_state,
        grad_scale,
        grad_gain,
        grad_weight_in,
        grad_bias_in,
        grad_weight_out,
        grad_bias_out,
    )


def solution(mesh):
    return jax.shard_map(
        local,
        mesh=mesh,
        in_specs=(
            P("member", "lat", None, None),
            P("member", "lat", None, None),
            P("member", None),
            P(),
            P(),
            P(),
            P(),
            P(),
            P(None, "lat", None, None),
            P(),
            P(),
        ),
        out_specs=(
            P(),
            P("member", "lat", None, None),
            P("member", "lat", None, None),
            P("member", None),
            P(),
            P(),
            P(),
            P(),
            P(),
        ),
        check_vma=False,
    )
```

profile of v0, /device:TPU:0, one launch (start us, length us, event | category | flops | bytes accessed | tf_op | source)
XLA Modules:
  0.0 2676.3 jit_solution(8913092405926765345)
XLA Ops:
  19.5 17.0 fusion.35
  36.6 24.4 copy.165
  68.2 133.2 %while.18 = (s32[]{:T(128)}, f32[12,96]{1,0:T(8,128)S(1)}, f32[12,96]{1,0:T(8,128)S(1)}, f32[91,12,96]{2,0,1:T(8,128)S(1)}, s32[91]{0:T(128)S(1)}, /*index=5*/f3...) while((s32[]{:T(128)}, f32[12,96]{1,0:T(8,128)S(1)}, ...), condition=%wide.region_6.7_spmd.clone, body=%wide.region_5.6_spmd.clone.sunk | while | flops 10478 | bytes 38395 | solution.py:54
  201.5 173.8 %all-to-all-done = f32[2,12,96,2,641]{4,3,1,0,2:T(2,128)} async-done(((f32[2,12,96,2,641]{4,3,1,0,2:T(2,128)}), f32[2,12,96,2,641]{4,3,1,0,2:T(2,128)}, u32[]{:S(2)}, u32[]{:S(2)}) %all-to-all-start) | async-done | bytes 11814944 | tf_op jit(solution)/shard_map/all_to_all | solution.py:134
  375.2 11.8 copy.167
  387.0 22.2 fusion.26
  409.3 16.7 fusion.31
  426.0 21.2 copy.171
  453.5 306.7 %all-to-all-done.1 = f32[2,96,12,2,641]{4,3,0,2,1:T(2,128)} async-done(((f32[2,96,12,2,641]{4,3,0,2,1:T(2,128)}), f32[2,96,12,2,641]{4,3,0,2,1:T(2,128)}, u32[]{:S(2)}, u32[]{:S(2)}) %all-to-all-start.1) | async-done | bytes 11814944 | tf_op jit(solution)/shard_map/all_to_all | solution.py:138
  760.2 12.1 copy.173
  772.3 23.4 bitcast_add_fusion.1
  795.7 13.8 reshape.515
  809.5 13.3 copy.175
  822.9 118.1 %fusion.5 = (f32[4320,1282]{0,1:T(8,128)}, f32[4320,1282]{0,1:T(8,128)}) fusion(f32[1282]{0:T(1024)S(1)} %copy-done.30, f32[4320,641]{1,0:T(8,128)} %reshape.515, f32[641,1282]{1,0:T(8,128)} %param.17), kind=kOutput, calls=%fused_computation.24 | convolution fusion | flops 42960134144 | bytes 58674576 | tf_op jit(solution)/shard_map/dot_general | solution.py:141
  941.0 64.1 %add_add_fusion = f32[4320,641]{0,1:T(8,128)} fusion(f32[4320,641]{0,1:T(8,128)S(1)} %copy-done.7, f32[4320,1282]{0,1:T(8,128)} %get-tuple-element.296, f32[1282,641]{0,1:T(8,128)S(1)} %copy-done.28, f32[641]{0:T(1024)S(1)} %copy-done.31), kind=kOutput, calls=%fused_computation.69 | convolution fusion | flops 42605682688 | bytes 47595532 | tf_op jit(solution)/shard_map/dot_general | solution.py:143
  1005.0 13.2 copy.176
  1018.2 14.0 reshape.516
  1032.2 11.0 broadcast_multiply_fusion
  1058.2 12.0 mini-gather-slice
  1099.2 347.1 %all-gather.2.cloned.1.call-done = f32[8,12,180,633]{3,2,1,0:T(8,128)} async-done(((f32[2,12,180,633]{3,2,1,0:T(8,128)}), f32[8,12,180,633]{3,2,1,0:T(8,128)}) %all-gather.2.cloned.1.call-update) | async-done | bytes 43752976 | tf_op jit(solution)/shard_map/all_gather | solution.py:148
  1446.4 12.1 mini-gather-slice.5
  1458.5 14.1 gather_fusion.5
  1472.5 18.1 mini-gather-slice.4
  1490.6 15.7 gather_fusion.4
  1506.3 39.5 %divide_reduce_fusion = (f32[2,12,180,633]{3,2,1,0:T(8,128)S(1)}, f32[2,12,180,633]{3,2,1,0:T(8,128)}) fusion(f32[8,12,180,249]{3,2,1,0:T(8,128)} %gather_fusion.5, f32[8,12,180,384]{3,2,1,0:T(8,128)} %gather_fusion.4, f32[2,12,180,633]{3,2,1,0:T(8,128)} %slice.24, pred[2,4]{1,0:T(4,128)(4,1)S(1)} %get-tuple-element.278), kind=kLoop, calls=%fused_computation.15 | loop fusion | flops 82036800 | bytes 76567688 | tf_op jit(solution)/shard_map/reduce_sum | solution.py:170
  1545.8 19.7 subtract_multiply_fusion
  1565.5 10.9 pad_reduce_fusion
  1576.4 13.9 reshape.518
  1590.2 13.3 copy.179
  1603.6 76.3 %fusion.95 = (f32[1282]{0:T(1024)S(1)}, f32[4320,1282]{0,1:T(8,128)}) fusion(f32[4320,1282]{0,1:T(8,128)} %get-tuple-element.297, f32[4320,641]{1,0:T(8,128)} %reshape.518, f32[1282,641]{0,1:T(8,128)} %param.19), kind=kOutput, calls=%fused_computation.201 | convolution fusion | flops 42655526912 | bytes 58674576 | tf_op jit(solution)/shard_map/tc,hc->th/dot_general | solution.py:177
  1679.9 63.1 %convolution_add_fusion.1 = f32[4320,641]{0,1:T(8,128)} fusion(f32[4320,641]{0,1:T(8,128)S(1)} %copy-done.6, f32[4320,1282]{0,1:T(8,128)} %get-tuple-element.299, f32[641,1282]{1,0:T(8,128)S(1)} %copy-done.29), kind=kOutput, calls=%fused_computation.70 | convolution fusion | flops 42602913792 | bytes 47592968 | tf_op jit(solution)/shard_map/th,ch->tc/dot_general | solution.py:183
  1743.0 13.2 copy.180
  1756.2 13.8 reshape.574
  1770.0 20.1 convolution_bitcast_fusion
  1790.1 20.7 copy.181
  1810.8 312.5 %all_to_all.72 = f32[2,12,96,2,641]{4,3,1,0,2:T(2,128)S(1)} all-to-all(f32[2,12,96,2,641]{4,3,1,0,2:T(2,128)S(1)} %copy.181), channel_id=1, replica_groups=mesh['member'=4,'lat'=8] {'lat'}, dimensions={2} | all-to-all | bytes 23629824 | tf_op jit(solution)/shard_map/all_to_all | solution.py:186
  2129.4 26.1 fusion.17
  2155.5 18.9 fusion.32
  2174.4 15.3 copy.186
  2195.3 94.1 %fusion.97 = f32[1282,641]{0,1:T(8,128)} fusion(f32[4320,1282]{0,1:T(8,128)} %get-tuple-element.296, f32[4320,641]{1,0:T(8,128)} %reshape.518), kind=kOutput, calls=%fused_computation.203 | convolution fusion | flops 42600144896 | bytes 36516488 | tf_op jit(solution)/shard_map/th,tc->hc/dot_general | solution.py:176
  2289.4 132.9 %fusion.96 = f32[641,1282]{1,0:T(8,128)} fusion(f32[4320,641]{1,0:T(8,128)} %reshape.515, f32[4320,1282]{0,1:T(8,128)} %get-tuple-element.299), kind=kOutput, calls=%fused_computation.202 | convolution fusion | flops 42600144896 | bytes 36516488 | tf_op jit(solution)/shard_map/tc,th->ch/dot_general | solution.py:181
  2424.4 19.7 copy.191
  2444.0 126.8 %all-reduce.1 = (f32[]{:T(128)}, f32[1282]{0:T(1024)}, f32[641]{0:T(1024)}) all-reduce(f32[]{:T(128)} %get-tuple-element.289, f32[1282]{0:T(1024)S(1)} %get-tuple-element.298, f32[641]{0:T(1024)S(1)} %copy-done.19), channel_id=1, replica_groups=mesh['member'=4,'lat'=8] {'member','lat'}, use_global_device_ids=true, to_apply=%region_10.11 | all-reduce | flops 1924 | bytes 15392 | tf_op jit(solution)/shard_map/psum | solution.py:202
  2570.9 14.0 reshape.519
  2585.5 12.1 copy.188
  2597.6 22.1 bitcast_add_fusion
  2625.1 13.3 copy.192
  2641.5 16.6 psum.50
  (669 shorter events, 169.9 us)
Async XLA Ops:
  15.2 4.4 copy-start.2
  15.6 21.0 copy-start.13
  15.6 756.6 %copy-start.11 = (f32[180,96,1]{1,0,2:T(8,128)}, f32[180,96,1]{1,0,2:T(8,128)S(1)}, u32[]{:S(2)}) copy-start(f32[180,96,1]{1,0,2:T(8,128)S(1)} %get-tuple-element.294) | copy-start | bytes 207364
  61.0 6.9 copy-start.26
  61.0 314.3 %all-to-all-start = ((f32[2,12,96,2,641]{4,3,1,0,2:T(2,128)}), f32[2,12,96,2,641]{4,3,1,0,2:T(2,128)}, u32[]{:S(2)}, u32[]{:S(2)}) async-start(f32[2,12,96,2,641]{4,3,1,0,2:T(2,128)} %copy.165), calls=%async_computation | async-start | bytes 28311552 | tf_op jit(solution)/shard_map/all_to_all | solution.py:134
  68.1 318.9 %copy-start.20 = (f32[96]{0:T(128)}, f32[96]{0:T(128)S(1)}, u32[]{:S(2)}) copy-start(f32[96]{0:T(128)S(1)} %get-tuple-element.292) | copy-start | bytes 1156
  201.4 207.9 %copy-start.3 = (f32[91,12,96]{2,0,1:T(8,128)}, f32[91,12,96]{2,0,1:T(8,128)S(1)}, u32[]{:S(2)}) copy-start(f32[91,12,96]{2,0,1:T(8,128)S(1)} %get-tuple-element.145) | copy-start | bytes 1257988
  201.5 207.8 %copy-start.17 = (f32[12]{0:T(128)}, f32[12]{0:T(128)S(1)}, u32[]{:S(2)}) copy-start(f32[12]{0:T(128)S(1)} %compare_convert_fusion.1) | copy-start | bytes 148
  387.0 22.3 copy-start.9
  409.3 16.7 copy-start.1
  447.2 313.0 %all-to-all-start.1 = ((f32[2,96,12,2,641]{4,3,0,2,1:T(2,128)}), f32[2,96,12,2,641]{4,3,0,2,1:T(2,128)}, u32[]{:S(2)}, u32[]{:S(2)}) async-start(f32[2,96,12,2,641]{4,3,0,2,1:T(2,128)} %copy.171), calls=%async_computation.1 | async-start | bytes 28311552 | tf_op jit(solution)/shard_map/all_to_all | solution.py:138
  452.7 993.7 %all-gather.2.cloned.1.call-start = ((), (), s32[]{:S(2)}) async-start(), calls=%async_computation.4 | async-start | bytes 56524800 | tf_op jit(solution)/shard_map/all_gather | solution.py:148
  452.7 319.5 %copy-start.24 = (f32[96]{0:T(128)}, f32[96]{0:T(128)S(1)}, u32[]{:S(2)}) copy-start(f32[96]{0:T(128)S(1)} %or_select_fusion) | copy-start | bytes 1156
  760.2 12.1 copy-start.5
  760.2 12.1 copy-start.14
  809.5 13.3 copy-start.30
  822.8 118.1 %copy-start.7 = (f32[4320,641]{0,1:T(8,128)S(1)}, f32[4320,641]{0,1:T(8,128)}, u32[]{:S(2)}) copy-start(f32[4320,641]{0,1:T(8,128)} %copy.175) | copy-start | bytes 33229444
  822.8 118.1 %copy-start.28 = (f32[1282,641]{0,1:T(8,128)S(1)}, f32[1282,641]{0,1:T(8,128)}, u32[]{:S(2)}) copy-start(f32[1282,641]{0,1:T(8,128)} %param.19) | copy-start | bytes 9861148
  822.8 118.1 %copy-start.31 = (f32[641]{0:T(1024)S(1)}, f32[641]{0:T(1024)}, u32[]{:S(2)}) copy-start(f32[641]{0:T(1024)} %param.20) | copy-start | bytes 7696
  1018.2 14.0 copy-start.22
  1052.3 17.8 copy-start
  1085.0 13.6 copy-start.27
  1603.5 76.3 %copy-start.6 = (f32[4320,641]{0,1:T(8,128)S(1)}, f32[4320,641]{0,1:T(8,128)}, u32[]{:S(2)}) copy-start(f32[4320,641]{0,1:T(8,128)} %copy.179) | copy-start | bytes 33229444
  1603.6 76.3 %copy-start.29 = (f32[641,1282]{1,0:T(8,128)S(1)}, f32[641,1282]{1,0:T(8,128)}, u32[]{:S(2)}) copy-start(f32[641,1282]{1,0:T(8,128)} %param.17) | copy-start | bytes 9861148
  1756.2 13.8 copy-start.12
  1756.2 13.8 copy-start.15
  1756.2 13.8 copy-start.25
  2123.3 6.1 copy-start.4
  2123.3 6.1 copy-start.18
  2129.4 26.1 copy-start.10
  2129.4 26.1 copy-start.21
  2189.7 395.8 %all-to-all-start.3 = ((f32[2,96,12,2,641]{4,3,0,2,1:T(2,128)}), f32[2,96,12,2,641]{4,3,0,2,1:T(2,128)}, u32[]{:S(2)}, u32[]{:S(2)}) async-start(f32[2,96,12,2,641]{4,3,0,2,1:T(2,128)} %copy.186), calls=%async_computation.3 | async-start | bytes 28311552 | tf_op jit(solution)/shard_map/all_to_all | solution.py:195
  2195.2 462.8 %all-reduce.5.cloned.1.call-start = ((), (), s32[]{:S(2)}) async-start(), calls=%async_computation.5 | async-start | bytes 15187968 | tf_op jit(solution)/shard_map/psum | solution.py:202
  2289.4 132.9 %copy-start.16 = (f32[2,12,180,8]{2,3,1,0:T(8,128)S(1)}, f32[2,12,180,8]{2,3,1,0:T(8,128)}, u32[]{:S(2)}) copy-start(f32[2,12,180,8]{2,3,1,0:T(8,128)} %param.14) | copy-start | bytes 414724
  2422.3 21.7 copy-start.19
  2597.6 22.1 copy-start.23
  2625.1 13.4 copy-start.8
Sparse Core Ops, SparseCore 0:
  1052.5 393.8 all-gather.1
  2422.4 233.7 all-reduce.4
where the time goes:
time: 2680 us
  waiting for transfers between devices  828 us (31%)
  matrix products  715 us (27%)
  local copies, waits for them, and re-layouts  474 us (18%)
  blocking collectives  456 us (17%)
  other arithmetic  104 us (4%)
  loops' own time  65.2 us (2%)
    all_gather x1, waiting for transfers between devices, local(): lax.all_gather(sample_prediction, 'member', axis=0, tiled=True)  347 us
    all_to_all x1, blocking collectives, local(): lax.all_to_all(back_rows, 'lat', split_axis=2, concat_axis=1, tiled=True)  312 us
    all_to_all x1, waiting for transfers between devices, local(): lax.all_to_all(synth_cols, 'lat', split_axis=1, concat_axis=2, tiled=True)  307 us
    all_to_all x1, waiting for transfers between devices, local(): lax.all_to_all(spectral_rows, 'lat', split_axis=2, concat_axis=1, tiled=T...  174 us
    dot_general x1, matrix products, local(): jnp.einsum('tc,th->ch', mixed_flat, grad_pre, precision=highest)  133 us
    psum x1, blocking collectives, local(): lax.psum((grad_weight_in_part, grad_bias_in_part, grad_weight_out_part, g...  127 us
    dot_general x1, matrix products, local(): hidden_pre = jnp.dot(mixed_flat, weight_in, precision=highest) + bias_in  118 us
    dot_general x1, matrix products, local(): jnp.einsum('th,tc->hc', activated, grad_out, precision=highest)  94.1 us
  transfers between devices with their start and end apart: 5, of which 3 were waited for; matrix products, arithmetic and copies ran while one was open for 16% of the time, Pallas kernels for 0%

commit v1 on v0

v1 whole, which is shorter than its diff:
```python
import functools
import math

import jax
import jax.numpy as jnp
import ml_dtypes
import numpy as np
from jax import lax
from jax.experimental import pallas as pl
from jax.experimental.pallas import tpu as pltpu
from jax.sharding import PartitionSpec as P

VARIABLE_COUNT = 633
LMAX = 90
NLAT = 90
NLON = 180
ENSEMBLE_SIZE = 4
DATES = 2

LANES = 128
VMEM_LIMIT = 56 * 1024 * 1024
F32 = jnp.float32
BF16 = jnp.bfloat16


def cost(microseconds):
    return pl.CostEstimate(
        flops=int(microseconds * 1.0e9), bytes_accessed=1000, transcendentals=0
    )


def legendre_np():
    colat = (np.arange(NLAT) + 0.5) * (math.pi / NLAT)
    cosine, log_sine = np.cos(colat), np.log(np.sin(colat))
    table = np.zeros((LMAX + 1, LMAX + 1, NLAT))
    for m in range(LMAX + 1):
        start = 0.5 * (
            math.log(2.0 * m + 1.0)
            - math.log(4.0 * math.pi)
            + math.lgamma(m + 0.5)
            - 0.5 * math.log(math.pi)
            - math.lgamma(m + 1.0)
        )
        table[m, m] = np.exp(start + m * log_sine)
        for l in range(m + 1, LMAX + 1):
            factor = math.sqrt((4.0 * l * l - 1.0) / (l * l - m * m))
            shrink = math.sqrt(((l - 1.0) ** 2 - m * m) / (4.0 * (l - 1.0) ** 2 - 1.0))
            before = table[m, l - 2] if l >= m + 2 else 0.0
            table[m, l] = factor * (cosine * table[m, l - 1] - shrink * before)
    return table


def unit_plan(devices):
    whole = LMAX // 2 * 2 - 1
    rows = 8
    while True:
        pairs = rows // 2 - 1
        left = max(0, whole - devices * pairs)
        if 2 + 2 * left <= devices:
            break
        rows += 8
    orders = np.zeros((devices, rows // 2), np.int32)
    units = {}
    for i in range(whole - left):
        d, j = i % devices, i // devices
        orders[d, j] = i + 1
        units[d * rows + 2 * j] = (i + 1, 0)
        units[d * rows + 2 * j + 1] = (i + 1, 1)
    singles = [(0, 0), (LMAX, 0)]
    for i in range(whole - left, whole):
        singles += [(i + 1, 0), (i + 1, 1)]
    for d, (m, p) in enumerate(singles):
        orders[d, pairs] = m
        units[d * rows + rows - 2] = (m, p)
    return rows, orders, units


def fourier_np(total, units, lon_count, lon_padded):
    forward = np.zeros((total, lon_padded))
    inverse = np.zeros((total, lon_padded))
    k = np.arange(lon_count)
    for at, (m, p) in units.items():
        angle = 2.0 * math.pi / lon_count * ((k * m) % lon_count)
        wave = np.cos(angle) if p == 0 else -np.sin(angle)
        doubling = 1.0 if m == 0 or 2 * m == lon_count else 2.0
        forward[at, :lon_count] = wave * (2.0 * math.pi / lon_count)
        inverse[at, :lon_count] = wave * doubling
    return forward.astype(np.float32), inverse.astype(np.float32)


def split_np(table):
    high = table.astype(ml_dtypes.bfloat16)
    low = (table - high.astype(np.float32)).astype(ml_dtypes.bfloat16)
    return jnp.asarray(high), jnp.asarray(low)


def split_x(table):
    high = lax.reduce_precision(table, 8, 7)
    return high.astype(BF16), (table - high).astype(BF16)


def split(value):
    high = value.astype(BF16)
    return high, (value - high.astype(F32)).astype(BF16)


def dot3(a, b):
    (ah, al), (bh, bl) = a, b
    dot = functools.partial(jnp.dot, preferred_element_type=F32)
    return dot(ah, bh) + (dot(ah, bl) + dot(al, bh))


def triple(value):
    high, low = split(value)
    return jnp.concatenate([high, high, low], axis=1)


def dot_triple(value, w_ref):
    w = w_ref[...].reshape(3 * w_ref.shape[1], w_ref.shape[2])
    return jnp.dot(triple(value), w, preferred_element_type=F32)


def params():
    return pltpu.CompilerParams(
        dimension_semantics=("arbitrary",), vmem_limit_bytes=VMEM_LIMIT
    )


def whole(shape):
    return pl.BlockSpec(shape, lambda i: (0,) * len(shape))


def diagonal(shape):
    return lax.broadcasted_iota(jnp.int32, shape, 1) == lax.broadcasted_iota(
        jnp.int32, shape, 2
    )


def analysis_body(shape, x, th_ref, tl_ref, o_ref):
    devices, rows, main = shape
    out = dot3((th_ref[...], tl_ref[...]), split(x))
    o_ref[...] = out[:, :main].reshape(devices, 1, rows, main)
    column = out[:, main : main + 1].reshape(devices, rows, 1)
    spare = jnp.where(diagonal((devices, rows, LANES)), column, 0.0).sum(axis=1)
    for d in range(devices):
        o_ref[d, 0, rows - 1 : rows, :LANES] = spare[d : d + 1, :]


def analysis_kernel(shape, x_ref, *refs):
    analysis_body(shape, x_ref[0], *refs)


def first_kernel(shape, part, state_ref, noise_ref, *refs):
    *tables, x_ref, o_ref, joined = refs
    lon, channels = state_ref.shape[1], state_ref.shape[3]
    base = channels // LANES * LANES

    @pl.when(pl.program_id(0) == 0)
    def _():
        joined[...] = jnp.zeros_like(joined)

    joined[:lon, :channels] = state_ref[0, :, part, :]
    lane = lax.broadcasted_iota(jnp.int32, noise_ref.shape[2:], 1)
    joined[:, base:] = jnp.where(lane < channels - base, joined[:, base:], noise_ref[0, 0])
    x = joined[...]
    x_ref[0] = x[:, : x_ref.shape[2]]
    analysis_body(shape, x, *tables, o_ref)


def analysis(x, first, row_count, table, plan, part=None):
    devices, rows, main = plan
    total, lon = table.shape
    th, tl = split_np(table)
    out_specs = [pl.BlockSpec((devices, 1, rows, main), lambda r: (0, r, 0, 0))]
    out_shape = [jax.ShapeDtypeStruct((devices, row_count, rows, main), F32)]
    scratch = []
    if part is None:
        kernel = functools.partial(analysis_kernel, plan)
        operands = [x]
        x_specs = [pl.BlockSpec((1, lon, main + 1), lambda r: (first + r, 0, 0))]
    else:
        kernel = functools.partial(first_kernel, plan, part)
        state, noise = operands = x
        x_specs = [
            pl.BlockSpec((1, *state.shape[1:]), lambda r: (r, 0, 0, 0)),
            pl.BlockSpec((1, 1, *noise.shape[2:]), lambda r: (part, r, 0, 0)),
        ]
        out_specs.insert(0, pl.BlockSpec((1, lon, main + 1), lambda r: (r, 0, 0)))
        out_shape.insert(0, jax.ShapeDtypeStruct((row_count, lon, main + 1), F32))
        scratch.append(pltpu.VMEM((lon, main + LANES), F32))
    return pl.pallas_call(
        kernel,
        grid=(row_count,),
        in_specs=x_specs + [whole((total, lon))] * 2,
        out_specs=out_specs,
        out_shape=out_shape,
        scratch_shapes=scratch,
        compiler_params=params(),
        cost_estimate=cost(1.2 * row_count),
        name="analysis",
    )(*operands, th, tl)


def synthesis_kernel(shape, joint, y_ref, th_ref, tl_ref, x_ref, *refs):
    devices, rows, main = shape
    *others, o_ref = refs
    total = devices * rows
    table = (th_ref[...], tl_ref[...])
    out = x_ref[0, :, :main] + dot3(table, split(y_ref[...].reshape(total, main)))
    if joint:
        lon, channels = o_ref.shape[1], o_ref.shape[3]
        for i, other in enumerate(others):
            o_ref[0, :, i, :] = other[0, :lon, :channels]
        o_ref[0, :, len(others), :] = out[:lon, :channels]
        return
    o_ref[0, :, :main] = out
    spare = y_ref[:, 0, rows - 1 : rows, :LANES]
    column = jnp.where(
        diagonal((devices, rows, LANES)), jnp.broadcast_to(spare, (devices, rows, LANES)), 0.0
    ).sum(axis=2, keepdims=True)
    column = jnp.broadcast_to(column.reshape(total, 1), (total, LANES))
    o_ref[0, :, main:] = x_ref[0, :, main:] + dot3(table, split(column))[:, :1]


def synthesis(y, table, x, first, held=None, joint=None):
    devices, row_count, rows, main = y.shape
    all_rows, lon, width = x.shape
    total = table.shape[0]
    th, tl = split_np(table.T.copy())
    x_spec = pl.BlockSpec((1, lon, width), lambda r: (first + r, 0, 0))
    operands = [y, th, tl, x]
    in_specs = [
        pl.BlockSpec((devices, 1, rows, main), lambda r: (0, r, 0, 0)),
        whole((lon, total)),
        whole((lon, total)),
        x_spec,
    ]
    out_spec, out_shape = x_spec, (all_rows, lon, width)
    aliases = {}
    if joint is not None:
        others, lon_out, channels = joint
        operands += others
        in_specs += [x_spec] * len(others)
        out_shape = (all_rows, lon_out, len(others) + 1, channels)
        out_spec = pl.BlockSpec((1, *out_shape[1:]), lambda r: (r, 0, 0, 0))
    elif held is not None:
        aliases = {len(operands): 0}
        operands.append(held)
        in_specs.append(pl.BlockSpec(memory_space=pl.ANY))
    return pl.pallas_call(
        functools.partial(synthesis_kernel, (devices, rows, main), joint is not None),
        grid=(row_count,),
        in_specs=in_specs,
        out_specs=out_spec,
        out_shape=jax.ShapeDtypeStruct(out_shape, F32),
        input_output_aliases=aliases,
        compiler_params=params(),
        cost_estimate=cost(1.2 * row_count),
        name="synthesis",
    )(*operands)


def halves(chains, rows):
    steps = len(chains[0][3])
    sizes = [rows >> k for k in range(steps + 1)]
    sides, starts = [], []
    for *_, order in chains:
        side, at = [], [0]
        for k, (axis, bit_at) in enumerate(order):
            me = lax.axis_index(axis)
            bit = (me // (1 << bit_at)) % 2
            side.append((bit, {axis: me + (1 - 2 * bit) * (1 << bit_at)}))
            at.append(at[-1] + bit * sizes[k + 1])
        sides.append(side)
        starts.append(at)
    return sides, starts, sizes


def greet(partners):
    barrier = pltpu.get_barrier_semaphore()
    for _, partner in partners:
        pl.semaphore_signal(
            barrier, inc=1, device_id=partner, device_id_type=pl.DeviceIdType.MESH
        )
    pl.semaphore_wait(barrier, len(partners))


def send_to(partner, source, target, send, recv):
    return pltpu.make_async_remote_copy(
        src_ref=source,
        dst_ref=target,
        send_sem=send,
        recv_sem=recv,
        device_id=partner,
        device_id_type=pl.DeviceIdType.MESH,
    )


def scatter_sum_kernel(chains, near, arrays, *refs):
    count, steps = len(chains), len(chains[0][3])
    ins, outs, refs = refs[:arrays], refs[arrays : 2 * arrays], refs[2 * arrays :]
    send, recv = refs[-2:]
    kept, landed = refs[:count], refs[count:-2]
    sides, starts, sizes = halves(chains, ins[0].shape[0])
    lanes = [pl.ds(first, size) for _, first, size, _ in chains]
    greet(sides[0])

    def halve(c, k):
        bit, partner = sides[c][k]
        give = starts[c][k] + (1 - bit) * sizes[k + 1]
        give = pl.ds(pl.multiple_of(give, 8), sizes[k + 1])
        source = ins[chains[c][0]].at[give, lanes[c]] if k == 0 else kept[c].at[give]
        return send_to(partner, source, landed[c * steps + k], send.at[c, k], recv.at[c, k])

    def share(c, k):
        return pl.ds(pl.multiple_of(starts[c][k] - starts[c][near], 8), sizes[k])

    def double(c, k):
        have = outs[chains[c][0]].at[share(c, k + 1), lanes[c]]
        step = 2 * steps - 1 - k
        return send_to(sides[c][k][1], have, have, send.at[c, step], recv.at[c, step])

    flying = []
    for c in range(count):
        flying.append(halve(c, 0))
        flying[c].start()
    for k in range(steps):
        for c in range(count):
            flying[c].wait()
            rows = pl.ds(pl.multiple_of(starts[c][k + 1], 8), sizes[k + 1])
            mine = ins[chains[c][0]][rows, lanes[c]] if k == 0 else kept[c][rows, :]
            total = mine + landed[c * steps + k][...]
            if k + 1 < steps:
                kept[c][rows, :] = total
                flying[c] = halve(c, k + 1)
            else:
                outs[chains[c][0]][share(c, steps), lanes[c]] = total
                flying[c] = double(c, k)
            flying[c].start()
    for k in reversed(range(near, steps)):
        for c in range(count):
            flying[c].wait()
            if k > near:
                flying[c] = double(c, k - 1)
                flying[c].start()


def gather_kernel(chains, near, arrays, *refs):
    count = len(chains)
    ins, outs, (send, recv) = refs[:arrays], refs[arrays : 2 * arrays], refs[2 * arrays :]
    sides, starts, sizes = halves(chains, outs[0].shape[0])
    lanes = [pl.ds(first, size) for _, first, size, _ in chains]
    greet(sides[0][:near])

    def double(c, k):
        rows = pl.ds(pl.multiple_of(starts[c][k + 1], 8), sizes[k + 1])
        have = outs[chains[c][0]].at[rows, lanes[c]]
        return send_to(sides[c][k][1], have, have, send.at[c, k], recv.at[c, k])

    flying = []
    for c in range(count):
        rows = pl.ds(pl.multiple_of(starts[c][near], 8), sizes[near])
        outs[chains[c][0]][rows, lanes[c]] = ins[chains[c][0]][:, lanes[c]]
        flying.append(double(c, near - 1))
        flying[c].start()
    for k in reversed(range(near)):
        for c in range(count):
            flying[c].wait()
            if k > 0:
                flying[c] = double(c, k - 1)
                flying[c].start()


def lane_chains(arrays, width, orders):
    cut = width // (2 * LANES) * LANES
    both = ((0, cut, orders[0]), (cut, width - cut, orders[1]))
    return [(i, *half) for i in range(arrays) for half in both]


def remote_params(collective_id):
    return pltpu.CompilerParams(
        collective_id=collective_id, has_side_effects=True, vmem_limit_bytes=VMEM_LIMIT
    )


def scatter_sum(xs, orders, near, collective_id):
    rows, width = xs[0].shape
    steps = len(orders[0])
    chains = lane_chains(len(xs), width, orders)
    vmem = pl.BlockSpec(memory_space=pltpu.VMEM)
    return pl.pallas_call(
        functools.partial(scatter_sum_kernel, chains, near, len(xs)),
        in_specs=[vmem] * len(xs),
        out_specs=[vmem] * len(xs),
        out_shape=[jax.ShapeDtypeStruct((rows >> near, width), F32)] * len(xs),
        scratch_shapes=[pltpu.VMEM((rows, size), F32) for _, _, size, _ in chains]
        + [
            pltpu.VMEM((rows >> (k + 1), size), F32)
            for _, _, size, _ in chains
            for k in range(steps)
        ]
        + [pltpu.SemaphoreType.DMA((len(chains), 2 * steps))] * 2,
        compiler_params=remote_params(collective_id),
        cost_estimate=cost(80),
        name="scatter_sum",
    )(*xs)


def gather(xs, orders, near, collective_id):
    rows, width = xs[0].shape
    chains = lane_chains(len(xs), width, orders)
    vmem = pl.BlockSpec(memory_space=pltpu.VMEM)
    return pl.pallas_call(
        functools.partial(gather_kernel, chains, near, len(xs)),
        in_specs=[vmem] * len(xs),
        out_specs=[vmem] * len(xs),
        out_shape=[jax.ShapeDtypeStruct((rows << near, width), F32)] * len(xs),
        scratch_shapes=[pltpu.SemaphoreType.DMA((len(chains), near))] * 2,
        compiler_params=remote_params(collective_id),
        cost_estimate=cost(40),
        name="gather",
    )(*xs)


def weights_kernel(hidden, main, a_ref, b_ref, *refs):
    for w_ref, (plain, flipped, e) in zip((a_ref, b_ref), (refs[:3], refs[3:])):
        w = w_ref[...]
        column = lax.broadcasted_iota(jnp.int32, w.shape, 1) + pl.program_id(0) * LANES
        w = jnp.where(column < hidden, w, 0.0)
        for ref, value in ((plain, w[:main]), (flipped, w[:main].T)):
            high, low = split(value)
            ref[0] = high
            ref[1] = low
            ref[2] = high
        e[...] = w[main : main + 1]


def prepare_weights(a, b):
    width, hidden = a.shape
    main = width // LANES * LANES
    tiles = (hidden + LANES - 1) // LANES
    across = pl.BlockSpec((3, main, LANES), lambda i: (0, 0, i))
    down = pl.BlockSpec((3, LANES, main), lambda i: (0, i, 0))
    row = pl.BlockSpec((1, LANES), lambda i: (0, i))
    total = tiles * LANES
    shapes = [
        jax.ShapeDtypeStruct((3, main, total), BF16),
        jax.ShapeDtypeStruct((3, total, main), BF16),
        jax.ShapeDtypeStruct((1, total), F32),
    ]
    out = pl.pallas_call(
        functools.partial(weights_kernel, hidden, main),
        grid=(tiles,),
        in_specs=[pl.BlockSpec((width, LANES), lambda i: (0, i))] * 2,
        out_specs=[across, down, row] * 2,
        out_shape=shapes * 2,
        compiler_params=params(),
        cost_estimate=cost(12),
        name="weights",
    )(a, b)
    return out[:3], out[3:]


def lane_mask(shape, j):
    lane = lax.broadcasted_iota(jnp.int32, shape, 1)
    return (lane == 2 * j) | (lane == 2 * j + 1)


def filter_kernel(shape, backward, *refs):
    in_sizes, out_sizes, rows = shape
    g_refs, refs = refs[: len(in_sizes)], refs[len(in_sizes) :]
    ah_ref, al_ref, bh_ref, bl_ref, gain_ref, egain_ref = refs[:6]
    refs = refs[6:]
    if backward:
        c_ref, ec_ref = refs[:2]
        refs = refs[2:]
    h_refs, refs = refs[: len(out_sizes)], refs[len(out_sizes) :]
    if backward:
        gg_ref, egg_ref = refs
    else:
        c_ref, ec_ref = refs
    tables = rows // 2
    slots = sum(out_sizes)

    def load(u):
        parts = [
            ref[pl.ds(u, n, stride=rows), :] for ref, n in zip(g_refs, in_sizes)
        ]
        return parts[0] if len(parts) == 1 else jnp.concatenate(parts, axis=0)

    def store(u, value):
        first = 0
        for ref, n in zip(h_refs, out_sizes):
            ref[pl.ds(u, n, stride=rows), :] = value[first : first + n, :]
            first += n

    gain = gain_ref[...]
    gain2 = jnp.concatenate([gain, gain], axis=1)
    total = jnp.zeros(gain.shape, F32)
    for j in range(tables):
        x = jnp.concatenate([load(2 * j), load(2 * j + 1)], axis=1)
        c = dot3((ah_ref[j], al_ref[j]), split(x))
        if backward:
            total += c_ref[2 * j] * c[:, :LANES]
            if j < tables - 1:
                total += c_ref[2 * j + 1] * c[:, LANES:]
        else:
            c_ref[2 * j] = c[:, :LANES]
            c_ref[2 * j + 1] = c[:, LANES:]
        y = dot3((bh_ref[j], bl_ref[j]), split(c * gain2))
        store(2 * j, y[:, :LANES])
        store(2 * j + 1, y[:, LANES:])
    if backward:
        gg_ref[...] = total

    @pl.when(pl.program_id(0) == 0)
    def _():
        x = split(load(rows - 1))
        c = jnp.zeros(gain.shape, F32)
        for j in range(tables):
            mine = dot3((ah_ref[j], al_ref[j]), x)
            c = jnp.where(lane_mask(c.shape, j), mine, c)
        if backward:
            egg_ref[...] = ec_ref[...] * c
        else:
            ec_ref[...] = c
        c = split(c * egain_ref[...])
        y = jnp.zeros((slots, LANES), F32)
        for j in range(tables):
            mine = dot3((bh_ref[j], bl_ref[j]), c)
            y = jnp.where(lane_mask(y.shape, j), mine, y)
        store(rows - 1, y)


def filter_slots(gs, first, second, gain, out_rows, coeffs=None):
    devices, _, rows, main = gs[0].shape
    in_sizes = [devices * g.shape[1] for g in gs]
    out_sizes = [devices * n for n in out_rows]
    slots = sum(in_sizes)
    degrees = first[0].shape[1]
    backward = coeffs is not None
    block = lambda n: pl.BlockSpec((n * rows, LANES), lambda t: (0, t))
    c_spec = pl.BlockSpec((rows, degrees, LANES), lambda t: (0, 0, t))
    ec_spec = whole((degrees, LANES))
    gg_spec = pl.BlockSpec((degrees, LANES), lambda t: (0, t))
    main_gain, extra_gain = gain
    in_specs = [block(n) for n in in_sizes] + [
        whole(first[0].shape),
        whole(first[0].shape),
        whole(second[0].shape),
        whole(second[0].shape),
        gg_spec,
        whole((degrees, 1)),
    ]
    operands = [g.reshape(-1, main) for g in gs]
    operands += [*first, *second, main_gain, extra_gain]
    out_shape = [jax.ShapeDtypeStruct((n * rows, main), F32) for n in out_sizes]
    out_specs = [block(n) for n in out_sizes]
    if backward:
        in_specs += [c_spec, ec_spec]
        operands += list(coeffs)
        out_shape.append(jax.ShapeDtypeStruct((degrees, main), F32))
        out_specs.append(gg_spec)
    else:
        out_shape.append(jax.ShapeDtypeStruct((rows, degrees, main), F32))
        out_specs.append(c_spec)
    out_shape.append(jax.ShapeDtypeStruct((degrees, LANES), F32))
    out_specs.append(ec_spec)
    *h, c, ec = pl.pallas_call(
        functools.partial(filter_kernel, (in_sizes, out_sizes, rows), backward),
        grid=(main // LANES,),
        in_specs=in_specs,
        out_specs=out_specs,
        out_shape=out_shape,
        compiler_params=params(),
        cost_estimate=cost(12),
        name="filter_back" if backward else "filter",
    )(*operands)
    h = [x.reshape(devices, n, rows, main) for x, n in zip(h, out_rows)]
    return h, (c, ec)


def mlp_kernel(main, m_ref, w1, w1e, b1, w2, w2e, b2, b2e, *refs):
    act_ref, slope_ref, out_ref, field_ref = refs[-4:]
    m = m_ref[:, :main]
    extra = m_ref[:, main:]
    v = dot_triple(m, w1) + extra * w1e[...] + b1[...]
    cdf = 0.5 * (1.0 + lax.erf(v * (1.0 / math.sqrt(2.0))))
    slope_ref[...] = cdf + v * jnp.exp(-0.5 * v * v) * (1.0 / math.sqrt(2.0 * math.pi))
    act = v * cdf
    act_ref[...] = act
    out = m + dot_triple(act, w2) + b2[...]
    out_ref[:, :main] = out
    field_ref[...] = out
    last = jnp.sum(act * w2e[...], axis=1, keepdims=True)
    out_ref[:, main:] = extra + last + b2e[...]


def tile_of(tokens, most):
    tile = most // 8 * 8
    while tokens % tile:
        tile -= 8
    return tile


def mlp(mixed, first, tokens, weights, held):
    whole_count, width = mixed.shape
    w1, w1e, b1, w2, w2e, b2, b2e = weights
    _, main, hidden = w1.shape
    tile = tile_of(math.gcd(first, tokens), 368)
    at = first // tile
    row = lambda n: pl.BlockSpec((tile, n), lambda i: (at + i, 0))
    shape = lambda n: jax.ShapeDtypeStruct((whole_count, n), F32)
    operands = [mixed, w1, w1e, b1, w2, w2e, b2, b2e]
    in_specs = [row(width)] + [whole(x.shape) for x in operands[1:]]
    aliases = {len(operands) + i: i for i in range(len(held))}
    return pl.pallas_call(
        functools.partial(mlp_kernel, main),
        grid=(tokens // tile,),
        in_specs=in_specs + [pl.BlockSpec(memory_space=pl.ANY)] * len(held),
        out_specs=(
            row(hidden),
            row(hidden),
            row(width),
            pl.BlockSpec((tile, main), lambda i: (i, 0)),
        ),
        out_shape=(
            shape(hidden),
            shape(hidden),
            shape(width),
            jax.ShapeDtypeStruct((tokens, main), F32),
        ),
        input_output_aliases=aliases,
        compiler_params=params(),
        cost_estimate=cost(0.023 * tokens),
        name="mlp",
    )(*operands, *held)


def mlp_back_kernel(main, g_ref, slope_ref, w2, w1, w1e, *refs):
    pre_ref, gm_ref, bias_in_ref, bias_out_ref = refs[-4:]

    @pl.when(pl.program_id(0) == 0)
    def _():
        bias_in_ref[...] = jnp.zeros_like(bias_in_ref)
        bias_out_ref[...] = jnp.zeros_like(bias_out_ref)

    g = g_ref[...]
    pre = dot_triple(g, w2) * slope_ref[...]
    pre_ref[...] = pre
    gm_ref[:, :main] = g + dot_triple(pre, w1)
    gm_ref[:, main:] = jnp.sum(pre * w1e[...], axis=1, keepdims=True)
    bias_in_ref[...] += jnp.sum(pre, axis=0, keepdims=True)
    bias_out_ref[...] += jnp.sum(g, axis=0, keepdims=True)


def mlp_back(g, slope, first, weights, held):
    tokens, main = g.shape
    whole_count, hidden = slope.shape
    w2, w1, w1e = weights
    tile = tile_of(math.gcd(first, tokens), 368)
    at = first // tile
    row = lambda n: pl.BlockSpec((tile, n), lambda i: (at + i, 0))
    shape = lambda n: jax.ShapeDtypeStruct((whole_count, n), F32)
    operands = [g, slope, w2, w1, w1e]
    in_specs = [pl.BlockSpec((tile, main), lambda i: (i, 0)), row(hidden)]
    in_specs += [whole(x.shape) for x in operands[2:]]
    aliases = {len(operands) + i: i for i in range(len(held))}
    return pl.pallas_call(
        functools.partial(mlp_back_kernel, main),
        grid=(tokens // tile,),
        in_specs=in_specs + [pl.BlockSpec(memory_space=pl.ANY)] * len(held),
        out_specs=(row(hidden), row(main + 1), whole((1, hidden)), whole((1, main))),
        out_shape=(
            shape(hidden),
            shape(main + 1),
            jax.ShapeDtypeStruct((1, hidden), F32),
            jax.ShapeDtypeStruct((1, main), F32),
        ),
        input_output_aliases=aliases,
        compiler_params=params(),
        cost_estimate=cost(0.021 * tokens),
        name="mlp_back",
    )(*operands, *held)


def crps_kernel(shape, groups_ref, *refs):
    own, sources, lane_tiles, channels = shape
    members = own * sources
    f_refs = refs[:members]
    t_ref, a_ref = refs[members : members + 2]
    g_refs = refs[members + 2 : 2 * members + 2]
    loss_ref, f_all, g_all = refs[2 * members + 2 :]
    pair_scale = 1.0 / (ENSEMBLE_SIZE * (ENSEMBLE_SIZE - 1))

    @pl.when(pl.program_id(0) == 0)
    def _():
        loss_ref[...] = jnp.zeros_like(loss_ref)

    def chunk(i, total):
        rows = pl.ds(pl.multiple_of(i * 8, 8), 8)
        area = jnp.broadcast_to(a_ref[rows, :], (8, LANES))
        for j in range(lane_tiles):
            lanes = slice(j * LANES, (j + 1) * LANES)
            weight = area
            if (j + 1) * LANES > channels:
                lane = lax.broadcasted_iota(jnp.int32, area.shape, 1)
                weight = jnp.where(lane + j * LANES < channels, area, 0.0)
            for source in range(sources):
                for b in range(own):
                    f_all[source * own + b] = f_refs[source * own + b][rows, lanes]
            for d in range(DATES):
                places = [groups_ref[d * ENSEMBLE_SIZE + i] for i in range(ENSEMBLE_SIZE)]
                f = [f_all[m] for m in places]
                observed = t_ref[d, rows, lanes]
                skill = jnp.zeros_like(area)
                couple = jnp.zeros_like(area)
                grads = []
                for v in f:
                    v = v - observed
                    square = v * v + 1.0
                    inverse = lax.rsqrt(square)
                    skill += square * inverse
                    grads.append(v * inverse * (1.0 / ENSEMBLE_SIZE))
                for m in range(ENSEMBLE_SIZE):
                    for n in range(m + 1, ENSEMBLE_SIZE):
                        v = f[m] - f[n]
                        square = v * v + 1.0
                        inverse = lax.rsqrt(square)
                        couple += square * inverse
                        v = v * inverse * pair_scale
                        grads[m] -= v
                        grads[n] += v
                total += weight * (skill * (1.0 / ENSEMBLE_SIZE) - couple * pair_scale)
                for m, grad in zip(places, grads):
                    g_all[m] = weight * grad
            for source in range(sources):
                for b in range(own):
                    g_refs[source * own + b][rows, lanes] = g_all[source * own + b]
        return total

    count = a_ref.shape[0] // 8
    loss_ref[...] += lax.fori_loop(0, count, chunk, jnp.zeros((8, LANES), F32))


def crps(fields, own, observed, area, places, channels):
    members = len(fields)
    points, main = fields[0].shape
    tile = points // 2 if points % 16 == 0 else points
    spec = pl.BlockSpec((tile, main), lambda i, g: (i, 0))
    *grads, loss = pl.pallas_call(
        functools.partial(crps_kernel, (own, members // own, main // LANES, channels)),
        grid_spec=pltpu.PrefetchScalarGridSpec(
            num_scalar_prefetch=1,
            grid=(points // tile,),
            in_specs=[spec] * members
            + [
                pl.BlockSpec((DATES, tile, main), lambda i, g: (0, i, 0)),
                pl.BlockSpec((tile, 1), lambda i, g: (i, 0)),
            ],
            out_specs=[spec] * members + [pl.BlockSpec((8, LANES), lambda i, g: (0, 0))],
            scratch_shapes=[pltpu.VMEM((members, 8, LANES), F32)] * 2,
        ),
        out_shape=[jax.ShapeDtypeStruct((points, main), F32)] * members
        + [jax.ShapeDtypeStruct((8, LANES), F32)],
        compiler_params=params(),
        cost_estimate=cost(0.045 * points),
        name="crps",
    )(places, *fields, observed, area)
    return grads, jnp.sum(loss)


def local(
    state_now,
    sample_random_maps,
    noise_scale,
    spec_gain,
    weight_in,
    bias_in,
    weight_out,
    bias_out,
    targets,
    date_of,
    row_slot,
):
    highest, high = lax.Precision.HIGHEST, lax.Precision.HIGH
    own, row_count, lon, channels = state_now.shape
    width, hidden = weight_in.shape
    main = width // LANES * LANES
    devices = lax.axis_size("lat")
    sources = lax.axis_size("member")
    lat_rank = lax.axis_index("lat")
    member_rank = lax.axis_index("member")
    slots = devices * row_count
    members = own * sources

    groups = [row_count // 3] * 3 if row_count % 3 == 0 else [row_count]
    starts = [sum(groups[:q]) for q in range(len(groups))]
    padded = (lon + 7) // 8 * 8
    while any(n * padded % (8 * sources) for n in groups):
        padded += 8
    points = [n * padded // sources for n in groups]

    rows, orders, units = unit_plan(devices)
    plan = (devices, rows, main)
    forward_table, inverse_table = fourier_np(devices * rows, units, lon, padded)
    degrees = (LMAX + 8) // 8 * 8
    full = np.zeros((LMAX + 1, degrees, NLAT), np.float32)
    full[:, : LMAX + 1] = legendre_np().astype(np.float32)
    mine = lax.dynamic_index_in_dim(jnp.asarray(full[orders]), lat_rank, 0, keepdims=False)
    sine = np.sin((np.arange(NLAT) + 0.5) * (math.pi / NLAT))
    geometry = jnp.asarray(
        np.stack(
            [np.ones(NLAT), math.pi / NLAT * sine, NLAT * sine / np.sum(sine)]
        ).astype(np.float32)
    )

    def low_tables(blocks):
        ids = np.arange(slots, dtype=np.int32).reshape(devices, row_count)
        ids = np.concatenate([ids[:, a : a + n].reshape(-1) for a, n in blocks])
        hits = (row_slot[:, None] == jnp.asarray(ids)[None, :]).astype(F32)
        quadrature = jnp.dot(geometry, hits, precision=highest)[1]
        table = jnp.einsum("jla,as->jls", mine, hits, precision=highest)
        weighted, plain = split_x(table * quadrature), split_x(table)
        flip = lambda pair: tuple(jnp.swapaxes(t, 1, 2) for t in pair)
        return weighted, plain, flip(weighted), flip(plain)

    in_full = low_tables([(0, row_count)])
    in_groups = low_tables(list(zip(starts, groups)))

    own_ids = lat_rank * row_count + jnp.arange(row_count, dtype=jnp.int32)
    hits_own = (row_slot[:, None] == own_ids[None, :]).astype(F32)
    used_own, _, area_own = jnp.dot(geometry, hits_own, precision=highest)
    gain = jnp.pad(spec_gain, ((0, degrees - LMAX - 1), (0, 0)))
    gain = (gain[:, :main], gain[:, main:])

    hidden_padded = (hidden + LANES - 1) // LANES * LANES
    pad_cols = lambda w: jnp.pad(w, ((0, 0), (0, hidden_padded - hidden)))
    w1_parts, w2t_parts = prepare_weights(weight_in, weight_out.T)
    forward_weights = (
        w1_parts[0],
        w1_parts[2],
        pad_cols(bias_in[None, :]),
        w2t_parts[1],
        w2t_parts[2],
        bias_out[None, :main],
        bias_out[None, main:],
    )
    backward_weights = (w2t_parts[0], w1_parts[1], w1_parts[2])

    base = channels // LANES * LANES
    noise = jnp.pad(
        noise_scale[:, None, None, :] * sample_random_maps,
        ((0, 0), (0, 0), (0, padded - lon), (channels - base, main + LANES - width)),
    )
    state = jnp.transpose(state_now, (1, 2, 0, 3))
    observed = jnp.pad(
        targets, ((0, 0), (0, 0), (0, padded - lon), (0, main - channels))
    )
    token_area = jnp.where(jnp.arange(padded)[None, :] < lon, area_own[:, None], 0.0)
    observed_share, area_share = [], []
    for a, n, size in zip(starts, groups, points):
        o = observed[:, a : a + n].reshape(DATES, n * padded, main)
        o = lax.dynamic_slice_in_dim(o, member_rank * size, size, axis=1)
        t = token_area[a : a + n].reshape(n * padded, 1)
        t = lax.dynamic_slice_in_dim(t, member_rank * size, size, axis=0)
        observed_share.append(o)
        area_share.append(t)
    by_date = jnp.argsort(date_of, stable=True).astype(jnp.int32)
    places = ((by_date // own) ^ member_rank) * own + by_date % own

    def tie(x, *tokens):
        return lax.optimization_barrier((x, tokens))[0]

    moved = []

    def to_owner(x):
        x = tie(x, *moved[-1:])
        moved.append(lax.all_to_all(x, "lat", split_axis=0, concat_axis=0, tiled=True))
        return moved[-1]

    def swap(x, distance):
        if distance == 0:
            return x
        pairs = [(i, i ^ distance) for i in range(sources)]
        return lax.ppermute(x, "member", pairs)

    def exchange(q, field):
        size = points[q]
        shares = []
        for distance in range(sources):
            share = lax.dynamic_slice_in_dim(
                field, (member_rank ^ distance) * size, size, axis=0
            )
            shares.append(swap(share, distance))
        return shares

    every = range(len(groups))
    final = own - 1

    inputs, spectra, synths, coeffs = [], [], [], []
    for b in range(own):
        if b > 0:
            state, noise = tie((state, noise), f)
        x, f = analysis((state, noise), 0, row_count, forward_table, plan, b)
        inputs.append(x)
        spectra.append(to_owner(f))
    prepared = (forward_weights, backward_weights, observed_share, area_share, places)
    for b in range(own):
        if b > 0:
            spectra[b] = tie(spectra[b], *h)
        if b == final:
            spectra[b], prepared = lax.optimization_barrier((spectra[b], prepared))
        h, c = filter_slots(
            [spectra[b]],
            in_full[0],
            in_groups[3] if b == final else in_full[3],
            gain,
            groups if b == final else [row_count],
        )
        coeffs.append(c)
        synths.append([to_owner(h[0])])
    forward_weights, backward_weights, observed_share, area_share, places = prepared

    mixed, held, shares = [None] * own, [[] for _ in range(own)], {}

    def mix(b, q, *tokens):
        first, y = (starts[q], synths[b][q]) if b == final else (0, synths[b][0])
        y = tie(y, *tokens)
        mixed[b] = synthesis(y, inverse_table, inputs[b], first, mixed[b])

    def forward(b, q, *tokens):
        m = tie(mixed[b], *tokens).reshape(row_count * padded, width)
        *held[b], field = mlp(
            m, starts[q] * padded, groups[q] * padded, forward_weights, held[b]
        )
        shares[b, q] = exchange(q, field)
        return field

    results, got = {}, {}
    losses = []

    def score(q, *tokens):
        fields = [shares[b, q][d] for d in range(sources) for b in range(own)]
        fields = tie(fields, *tokens)
        out, part = crps(fields, own, observed_share[q], area_share[q], places, channels)
        losses.append(part)
        results[q] = out
        if q != 1:
            got[0, q] = returned(0, q)
        return out[0]

    def returned(b, q):
        return [swap(results[q][d * own + b], d) for d in range(sources)]

    def gradient(b, parts):
        size = sum(groups[q] for q in parts) * padded
        g = jnp.zeros((size, main), F32)
        for q in parts:
            for distance, share in enumerate(got[b, q]):
                at = (member_rank ^ distance) * points[q]
                at += (starts[q] - starts[parts[0]]) * padded
                g = lax.dynamic_update_slice_in_dim(g, share, at, axis=0)
        return g

    grads = [[] for _ in range(own)]
    slopes, back_held = {}, [[] for _ in range(own)]
    bias_in_sums, bias_out_sums = [], []
    back = [[] for _ in range(own)]

    def backward(b, q, *tokens):
        g = tie(gradient(b, [q]), *tokens)
        *back_held[b], b1, b2 = mlp_back(
            g, held[b][1], starts[q] * padded, backward_weights, back_held[b]
        )
        grads[b].append(g)
        bias_in_sums.append(b1)
        bias_out_sums.append(b2)
        return b2

    def send_back(b, parts):
        gm = tie(back_held[b][1], *moved[-1:]) if b > 0 or parts[0] > 0 else back_held[b][1]
        gm = gm.reshape(row_count, padded, width)
        size = sum(groups[q] for q in parts)
        f = analysis(gm, starts[parts[0]], size, inverse_table, plan)[0]
        back[b].append(to_owner(f))
        return f

    token = ()
    for b in range(final):
        mix(b, 0, *token)
        for q in every:
            token = (forward(b, q, *token),)
            if b == final - 1 and q == 1:
                synths[final].append(to_owner(tie(h[1], *token)))
    ready = lambda q: [shares[b, q] for b in range(final)]
    if len(groups) == 3:
        for q in (0, 1):
            mix(final, q, ready(q), *token)
            token = (forward(final, q),)
            if q == 0:
                synths[final].append(to_owner(tie(h[2], *token)))
        token = (score(0, ready(2), *token),)
        token = (score(1, *token),)
        first_back = backward(0, 0, synths[final][2], *token)
        results[1] = tie(results[1], first_back)
        got[0, 1] = returned(0, 1)
        for b in range(1, own):
            results[0] = tie(results[0], got[0, 1])
            got[b, 0] = returned(b, 0)
        token = (send_back(0, [0]),)
        mix(final, 2, *token)
        token = (forward(final, 2),)
        backward(0, 1, *token)
        token = (send_back(0, [1]),)
        token = (score(2, *token),)
        for b in range(1, own):
            token = (backward(b, 0, *token),)
            results[1] = tie(results[1], got[0, 2])
            got[b, 1] = returned(b, 1)
            results[2] = tie(results[2], got[b, 1])
            got[b, 2] = returned(b, 2)
        backward(0, 2, *token)
        token = (send_back(0, [2]),)
        for b in range(1, own):
            token = (backward(b, 1, *token),)
            token = (backward(b, 2, *token),)
            token = (send_back(b, list(every)),)
    else:
        for q in every:
            mix(final, q, *token)
            token = (forward(final, q),)
        for q in every:
            token = (score(q, *token),)
        for b in range(own):
            for q in every:
                if b > 0 or q == 1:
                    got[b, q] = returned(b, q)
                token = (backward(b, q, *token),)
            token = (send_back(b, list(every)),)
    loss = sum(losses)
    mixed = [m.reshape(row_count * padded, width) for m in mixed]
    act = [h[0] for h in held]
    block = [h[2] for h in held]
    g_pre = [h[0] for h in back_held]
    g_mixed = [h[1] for h in back_held]

    grads = tie(grads, *token)
    grad_out_t = 0.0
    for b in range(own):
        at = 0
        for g in grads[b]:
            n = g.shape[0]
            grad_out_t += jnp.einsum("tc,th->ch", g, act[b][at : at + n], precision=high)
            at += n
    g_pre = tie(g_pre, *token)
    grad_in = sum(
        jnp.einsum("tc,th->ch", mixed[b], g_pre[b], precision=high) for b in range(own)
    )
    grad_bias_in = sum(bias_in_sums)[0, :hidden]
    grad_bias_out = jnp.pad(sum(bias_out_sums)[0], (0, width - main))

    back[0], grad_out_t, grad_in = lax.optimization_barrier((back[0], grad_out_t, grad_in))
    spreads = []
    gain_by_member = []
    for b in range(own):
        split_in = len(back[b]) > 1
        (h,), (gg, egg) = filter_slots(
            back[b],
            in_groups[1] if split_in else in_full[1],
            in_full[2],
            gain,
            [row_count],
            coeffs[b],
        )
        if b == final:
            last_filtered = h
        else:
            spreads.append(to_owner(h))
        low = jnp.concatenate([gg, jnp.sum(egg, axis=1, keepdims=True)], axis=1)
        gain_by_member.append(low[: LMAX + 1])
    grad_gain = sum(gain_by_member)

    scale_parts = []
    for b in range(own):
        gm = g_mixed[b].reshape(row_count, padded, width)[:, :lon, channels:]
        direct = jnp.sum(gm * sample_random_maps[b], axis=(0, 1))
        spectral = jnp.sum(
            spec_gain[:, channels:] * gain_by_member[b][:, channels:], axis=0
        )
        scale_parts.append(direct + spectral / noise_scale[b])
    noise_count = width - channels
    scale_row = lax.dynamic_update_slice(
        jnp.zeros((members * noise_count,), F32),
        jnp.concatenate(scale_parts),
        (member_rank * own * noise_count,),
    )
    line = lambda v: jnp.pad(v, (0, -v.shape[0] % width)).reshape(-1, width)
    small = [grad_bias_out, grad_bias_in, jnp.concatenate([loss[None], scale_row])]
    small = [line(v) for v in small]
    pack = jnp.concatenate([grad_gain] + small, axis=0)
    bits = [("lat", 0), ("member", 0), ("member", 1)]
    bits += [("lat", k) for k in range(1, devices.bit_length() - 1)]
    if sources == 4 and len(bits) <= 5:
        lanes = hidden_padded
        flat = pack.reshape(-1)
        flat = jnp.pad(flat, (0, -flat.shape[0] % lanes)).reshape(-1, lanes)
        unit = 8 << len(bits)
        size = -(-(width + flat.shape[0]) // unit) * unit
        first = jnp.concatenate([grad_in, flat])
        arrays = [jnp.pad(x, ((0, size - x.shape[0]), (0, 0))) for x in (first, grad_out_t)]
        orders = [bits, [bits[0], bits[2], bits[1]] + bits[3:]]
        arrays = scatter_sum(tie(arrays, last_filtered), orders, 3, 1)
        last_filtered, arrays = lax.optimization_barrier((last_filtered, arrays))
        arrays = gather(tie(arrays, *spreads), orders, 3, 2)
        block, (first, second) = lax.optimization_barrier((block, arrays))
        grad_in, grad_out_t = first[:width, :hidden], second[:main, :hidden]
        flat = first[width : width + flat.shape[0]].reshape(-1)
        pack = flat[: pack.size].reshape(pack.shape)
    else:
        grad_in, grad_out_t, pack = lax.psum(
            (grad_in[:, :hidden], grad_out_t[:, :hidden], pack), ("member", "lat")
        )
    layer_output = jnp.stack(
        [x.reshape(row_count, padded, width)[:, :lon] for x in block]
    ) * used_own[None, :, None, None]
    done = []
    spreads.append(to_owner(last_filtered))
    for b in range(own):
        done.append(
            synthesis(
                tie(spreads[b], *done),
                forward_table,
                g_mixed[b].reshape(row_count, padded, width),
                0,
                joint=(done, lon, channels) if b == final else None,
            )
        )
    grad_state = jnp.transpose(done[-1], (2, 0, 1, 3))
    at = LMAX + 1
    grad_gain = pack[:at]
    grad_bias_out = pack[at]
    after = at + 1 + small[1].shape[0]
    grad_bias_in = pack[at + 1 : after].reshape(-1)[:hidden]
    last_row = pack[after:].reshape(-1)
    crps_loss = last_row[0] / (DATES * NLAT * NLON * channels)
    grad_scale = lax.dynamic_slice_in_dim(
        last_row, 1 + member_rank * own * noise_count, own * noise_count
    ).reshape(own, noise_count)
    grad_weight_out = jnp.pad(grad_out_t, ((0, width - main), (0, 0))).T

    return (
        crps_loss,
        layer_output,
        grad_state,
        grad_scale,
        grad_gain,
        grad_in,
        grad_bias_in,
        grad_weight_out,
        grad_bias_out,
    )


def solution(mesh):
    return jax.shard_map(
        local,
        mesh=mesh,
        in_specs=(
            P("member", "lat", None, None),
            P("member", "lat", None, None),
            P("member", None),
            P(),
            P(),
            P(),
            P(),
            P(),
            P(None, "lat", None, None),
            P(),
            P(),
        ),
        out_specs=(
            P(),
            P("member", "lat", None, None),
            P("member", "lat", None, None),
            P("member", None),
            P(),
            P(),
            P(),
            P(),
            P(),
        ),
        check_vma=False,
    )
```

time: 2680 us -> 1350 us (0.50)
  matrix products: 715 us -> 95.6 us
  Pallas kernels: 0 us -> 582 us
  blocking collectives: 456 us -> 0 us
  waiting for transfers between devices: 828 us -> 406 us
  local copies, waits for them, and re-layouts: 474 us -> 121 us
  starting transfers between devices: 17.8 us -> 103 us
  other arithmetic: 104 us -> 28.8 us
  loops' own time: 65.2 us -> 0 us
    dot_general x14 -> x12, matrix products: 715 us -> 95.6 us  [the longest x6 49.2 us: local(): grad_out_t += jnp.einsum('tc,th->ch', g, act[b][at:at + n], precision=high)]
    pallas_call x0 -> x34, Pallas kernels: none -> 582 us  [the longest x1 133 us: scatter_sum(): pl.pallas_call(functools.partial(scatter_sum_kernel, chains, near, len(xs...]
    all_gather x1 -> x0, waiting for transfers between devices: 347 us -> none  [local(): lax.all_gather(sample_prediction, 'member', axis=0, tiled=True)]
    all_to_all x1 -> x0, blocking collectives: 312 us -> none  [local(): lax.all_to_all(back_rows, 'lat', split_axis=2, concat_axis=1, tiled=True)]
    psum x2 -> x0, blocking collectives: 143 us -> none  [the longest x1 127 us: local(): lax.psum((grad_weight_in_part, grad_bias_in_part, grad_weight_out_part, g...]
    all_to_all x3 -> x12, waiting for transfers between devices: 480 us -> 358 us  [to_owner(): lax.all_to_all(x, 'lat', split_axis=0, concat_axis=0, tiled=True)]
    reshape x8 -> x10, local copies, waits for them, and re-layouts: 96.1 us -> 1.69 us  [the longest x1 0.64 us: local(): grad_scale = lax.dynamic_slice_in_dim(last_row, 1 + member_rank * own * n...]
    gather x10 -> x0, local copies, waits for them, and re-layouts: 91.4 us -> none  [the longest x4 59.9 us: local(): jnp.take(whole_ensemble_collected, mates.reshape(-1), axis=0)]
  transfers between devices with their start and end apart: 5 -> 48, of which waited for: 3 -> 14; matrix products, arithmetic and copies ran while one was open for 16% -> 17% of each run, Pallas kernels for 0% -> 37%
where the time goes in v1:
time: 1350 us; the launch traced here: 1340 us
  Pallas kernels  582 us (43%)
  waiting for transfers between devices  406 us (30%)
  local copies, waits for them, and re-layouts  121 us (9%)
  starting transfers between devices  103 us (8%)
  matrix products  95.6 us (7%)
  other arithmetic  28.8 us (2%)
    all_to_all x12, waiting for transfers between devices, to_owner(): lax.all_to_all(x, 'lat', split_axis=0, concat_axis=0, tiled=True)  358 us
    pallas_call x1, Pallas kernels, scatter_sum(): pl.pallas_call(functools.partial(scatter_sum_kernel, chains, near, len(xs...  133 us
    pallas_call x6, Pallas kernels, mlp(): pl.pallas_call(functools.partial(mlp_kernel, main), grid=(tokens // tile,...  103 us
    pallas_call x6, Pallas kernels, mlp_back(): pl.pallas_call(functools.partial(mlp_back_kernel, main), grid=(tokens //...  97.4 us
    all_to_all x12, starting transfers between devices, to_owner(): lax.all_to_all(x, 'lat', split_axis=0, concat_axis=0, tiled=True)  60.3 us
    pallas_call x6, Pallas kernels, analysis(): pl.pallas_call(kernel, grid=(row_count,), in_specs=x_specs + [whole((tota...  58.3 us
    pallas_call x6, Pallas kernels, synthesis(): pl.pallas_call(functools.partial(synthesis_kernel, (devices, rows, main),...  58.2 us
    dot_general x6, matrix products, local(): grad_out_t += jnp.einsum('tc,th->ch', g, act[b][at:at + n], precision=high)  49.2 us
  transfers between devices with their start and end apart: 48, of which 14 were waited for; matrix products, arithmetic and copies ran while one was open for 17% of the time, Pallas kernels for 37%

profile of v1, /device:TPU:0, one launch (start us, length us, event | category | flops | bytes accessed | tf_op | source)
XLA Modules:
  0.0 1341.8 jit_solution(8807207545330406122)
XLA Ops:
  6.5 15.2 %analysis.6 = (f32[12,184,641]{2,1,0:T(8,128)}, f32[8,12,24,640]{3,2,1,0:T(8,128)}) custom-call(f32[12,180,2,633]{3,2,1,0:T(2,128)} %bitcast.144, f32[2,12,184,256]{3,2,1,0:T(8,128)} %pad.40.noise_ref, bf16[192,184]{1,0:T(8,128)(2,1)} %constant.96.clone.refs_0_, bf16[192,184]{1,0:T(8,128)(2,1)} %constant.97.clone.refs_1_), custom_call_target="tpu_custom_call" | custom-call | flops 14400000000 | bytes 1000 | tf_op jit(solution)/shard_map/analysis/pallas_call | solution.py:191
  28.1 15.3 %analysis.7 = (f32[12,184,641]{2,1,0:T(8,128)}, f32[8,12,24,640]{3,2,1,0:T(8,128)}) custom-call(f32[12,180,2,633]{3,2,1,0:T(2,128)} %bitcast.145, f32[2,12,184,256]{3,2,1,0:T(8,128)} %pad.40.noise_ref, bf16[192,184]{1,0:T(8,128)(2,1)} %constant.96.clone.refs_0_, bf16[192,184]{1,0:T(8,128)(2,1)} %constant.97.clone.refs_1_), custom_call_target="tpu_custom_call" | custom-call | flops 14400000000 | bytes 1000 | tf_op jit(solution)/shard_map/analysis/pallas_call | solution.py:191
  43.3 115.4 %all-to-all-done = f32[8,12,24,640]{3,2,1,0:T(8,128)} async-done(((f32[8,12,24,640]{3,2,1,0:T(8,128)}), f32[8,12,24,640]{3,2,1,0:T(8,128)}, u32[]{:S(2)}, u32[]{:S(2)}) %all-to-all-start) | async-done | bytes 5898272 | tf_op jit(solution)/shard_map/all_to_all | solution.py:879
  168.6 11.9 filter.2
  180.5 113.6 %all-to-all-done.1 = f32[8,12,24,640]{3,2,1,0:T(8,128)} async-done(((f32[8,12,24,640]{3,2,1,0:T(8,128)}), f32[8,12,24,640]{3,2,1,0:T(8,128)}, u32[]{:S(2)}, u32[]{:S(2)}) %all-to-all-start.1) | async-done | bytes 5898272 | tf_op jit(solution)/shard_map/all_to_all | solution.py:879
  300.3 6.7 pad_slice_fusion
  327.0 11.9 weights.1
  338.9 11.8 filter.3
  350.7 79.0 %all-to-all-done.2.y_ref = f32[8,12,24,640]{3,2,1,0:T(8,128)} async-done(((f32[8,12,24,640]{3,2,1,0:T(8,128)}), f32[8,12,24,640]{3,2,1,0:T(8,128)}, u32[]{:S(2)}, u32[]{:S(2)}) %all-to-all-start.2) | async-done | bytes 5898272 | tf_op jit(solution)/shard_map/all_to_all | solution.py:879
  433.6 13.0 synthesis.6
  446.6 17.1 %mlp.6 = (f32[2208,1408]{1,0:T(8,128)}, f32[2208,1408]{1,0:T(8,128)}, f32[2208,641]{1,0:T(8,128)}, f32[736,640]{1,0:T(8,128)}) custom-call(f32[2208,641]{1,0:T(8,128)} %bitcast.148, bf16[3,640,1408]{2,1,0:T(8,128)(2,1)} %get-tuple-element.246.w1, f32[1,1408]{1,0:T(1,128)} %get-tuple-element.312.w1e, f32[1,1408]{1,0:T(1,128)} %pad.42.b1, ...), custom_call_target="tpu_custom_call" | custom-call | flops 16928000000 | bytes 1000 | tf_op jit(solution)/shard_map/mlp/pallas_call | solution.py:617
  463.7 17.3 %mlp.7 = (f32[2208,1408]{1,0:T(8,128)}, f32[2208,1408]{1,0:T(8,128)}, f32[2208,641]{1,0:T(8,128)}, f32[736,640]{1,0:T(8,128)}) custom-call(f32[2208,641]{1,0:T(8,128)} %bitcast.149, bf16[3,640,1408]{2,1,0:T(8,128)(2,1)} %get-tuple-element.246.w1, f32[1,1408]{1,0:T(1,128)} %get-tuple-element.312.w1e, ...), custom_call_target="tpu_custom_call", output_to_operand_aliasing={{0}: (8, {}), {1}: (9, {}), {2}: (10, {})} | custom-call | flops 16928000000 | bytes 1000 | tf_op jit(solution)/shard_map/mlp/pallas_call | solution.py:617
  492.6 17.1 %mlp.8 = (f32[2208,1408]{1,0:T(8,128)}, f32[2208,1408]{1,0:T(8,128)}, f32[2208,641]{1,0:T(8,128)}, f32[736,640]{1,0:T(8,128)}) custom-call(f32[2208,641]{1,0:T(8,128)} %bitcast.150, bf16[3,640,1408]{2,1,0:T(8,128)(2,1)} %get-tuple-element.246.w1, f32[1,1408]{1,0:T(1,128)} %get-tuple-element.312.w1e, ...), custom_call_target="tpu_custom_call", output_to_operand_aliasing={{0}: (8, {}), {1}: (9, {}), {2}: (10, {})} | custom-call | flops 16928000000 | bytes 1000 | tf_op jit(solution)/shard_map/mlp/pallas_call | solution.py:617
  525.1 17.1 %mlp.9 = (f32[2208,1408]{1,0:T(8,128)}, f32[2208,1408]{1,0:T(8,128)}, f32[2208,641]{1,0:T(8,128)}, f32[736,640]{1,0:T(8,128)}) custom-call(f32[2208,641]{1,0:T(8,128)} %bitcast.109, bf16[3,640,1408]{2,1,0:T(8,128)(2,1)} %get-tuple-element.246.w1, f32[1,1408]{1,0:T(1,128)} %get-tuple-element.312.w1e, f32[1,1408]{1,0:T(1,128)} %pad.42.b1, ...), custom_call_target="tpu_custom_call" | custom-call | flops 16928000000 | bytes 1000 | tf_op jit(solution)/shard_map/mlp/pallas_call | solution.py:617
  560.9 17.1 %mlp.10 = (f32[2208,1408]{1,0:T(8,128)}, f32[2208,1408]{1,0:T(8,128)}, f32[2208,641]{1,0:T(8,128)}, f32[736,640]{1,0:T(8,128)}) custom-call(f32[2208,641]{1,0:T(8,128)} %bitcast.110, bf16[3,640,1408]{2,1,0:T(8,128)(2,1)} %get-tuple-element.246.w1, f32[1,1408]{1,0:T(1,128)} %get-tuple-element.312.w1e, ...), custom_call_target="tpu_custom_call", output_to_operand_aliasing={{0}: (8, {}), {1}: (9, {}), {2}: (10, {})} | custom-call | flops 16928000000 | bytes 1000 | tf_op jit(solution)/shard_map/mlp/pallas_call | solution.py:617
  578.1 7.9 collective-permute-done.5.refs_7_
  592.0 8.7 crps.3
  612.3 10.1 collective-permute-done.12
  623.2 8.2 collective-permute-done.13
  633.1 8.7 crps.4
  641.8 16.8 %mlp_back.6 = (f32[2208,1408]{1,0:T(8,128)}, f32[2208,641]{1,0:T(8,128)}, f32[1,1408]{1,0:T(1,128)}, f32[1,640]{1,0:T(1,128)}) custom-call(f32[736,640]{1,0:T(8,128)} %constant_dynamic-update-slice_fusion.20.g_ref, f32[2208,1408]{1,0:T(8,128)} %get-tuple-element.309.slope_ref, bf16[3,640,1408]{2,1,0:T(8,128)(2,1)} %get-tuple-element.310.w2, ...), custom_call_target="tpu_custom_call" | custom-call | flops 15456000000 | bytes 1000 | tf_op jit(solution)/shard_map/mlp_back/pallas_call | solution.py:669
  676.5 17.1 %mlp.11 = (f32[2208,1408]{1,0:T(8,128)}, f32[2208,1408]{1,0:T(8,128)}, f32[2208,641]{1,0:T(8,128)}, f32[736,640]{1,0:T(8,128)}) custom-call(f32[2208,641]{1,0:T(8,128)} %bitcast.111, bf16[3,640,1408]{2,1,0:T(8,128)(2,1)} %get-tuple-element.246.w1, f32[1,1408]{1,0:T(1,128)} %get-tuple-element.312.w1e, ...), custom_call_target="tpu_custom_call", output_to_operand_aliasing={{0}: (8, {}), {1}: (9, {}), {2}: (10, {})} | custom-call | flops 16928000000 | bytes 1000 | tf_op jit(solution)/shard_map/mlp/pallas_call | solution.py:617
  705.4 16.1 %mlp_back.7 = (f32[2208,1408]{1,0:T(8,128)}, f32[2208,641]{1,0:T(8,128)}, f32[1,1408]{1,0:T(1,128)}, f32[1,640]{1,0:T(1,128)}) custom-call(f32[736,640]{1,0:T(8,128)} %copy-done.11, f32[2208,1408]{1,0:T(8,128)} %get-tuple-element.309.slope_ref, bf16[3,640,1408]{2,1,0:T(8,128)(2,1)} %get-tuple-element.310.w2, ...), custom_call_target="tpu_custom_call", output_to_operand_aliasing={{0}: (5, {}), {1}: (6, {})} | custom-call | flops 15456000000 | bytes 1000 | tf_op jit(solution)/shard_map/mlp_back/pallas_call | solution.py:669
  725.7 15.2 %collective-permute-done.34 = f32[184,640]{1,0:T(8,128)S(1)} collective-permute-done((f32[184,640]{1,0:T(8,128)S(1)}, f32[184,640]{1,0:T(8,128)S(1)}, u32[]{:S(2)}, u32[]{:S(2)}) %collective-permute-start.34) | collective-permute-done | bytes 471072 | tf_op jit(solution)/shard_map/ppermute | solution.py:886
  747.9 8.6 crps.5
  765.3 16.2 %mlp_back.8 = (f32[2208,1408]{1,0:T(8,128)}, f32[2208,641]{1,0:T(8,128)}, f32[1,1408]{1,0:T(1,128)}, f32[1,640]{1,0:T(1,128)}) custom-call(f32[736,640]{1,0:T(8,128)} %constant_dynamic-update-slice_fusion.g_ref, f32[2208,1408]{1,0:T(8,128)} %get-tuple-element.376.slope_ref, bf16[3,640,1408]{2,1,0:T(8,128)(2,1)} %get-tuple-element.310.w2, ...), custom_call_target="tpu_custom_call" | custom-call | flops 15456000000 | bytes 1000 | tf_op jit(solution)/shard_map/mlp_back/pallas_call | solution.py:669
  789.5 16.1 %mlp_back.9 = (f32[2208,1408]{1,0:T(8,128)}, f32[2208,641]{1,0:T(8,128)}, f32[1,1408]{1,0:T(1,128)}, f32[1,640]{1,0:T(1,128)}) custom-call(f32[736,640]{1,0:T(8,128)} %copy-done.13, f32[2208,1408]{1,0:T(8,128)} %get-tuple-element.309.slope_ref, bf16[3,640,1408]{2,1,0:T(8,128)(2,1)} %get-tuple-element.310.w2, ...), custom_call_target="tpu_custom_call", output_to_operand_aliasing={{0}: (5, {}), {1}: (6, {})} | custom-call | flops 15456000000 | bytes 1000 | tf_op jit(solution)/shard_map/mlp_back/pallas_call | solution.py:669
  831.7 16.1 %mlp_back.10 = (f32[2208,1408]{1,0:T(8,128)}, f32[2208,641]{1,0:T(8,128)}, f32[1,1408]{1,0:T(1,128)}, f32[1,640]{1,0:T(1,128)}) custom-call(f32[736,640]{1,0:T(8,128)} %constant_dynamic-update-slice_fusion.8.g_ref, f32[2208,1408]{1,0:T(8,128)} %get-tuple-element.376.slope_ref, ...), custom_call_target="tpu_custom_call", output_to_operand_aliasing={{0}: (5, {}), {1}: (6, {})} | custom-call | flops 15456000000 | bytes 1000 | tf_op jit(solution)/shard_map/mlp_back/pallas_call | solution.py:669
  847.8 16.1 %mlp_back.11 = (f32[2208,1408]{1,0:T(8,128)}, f32[2208,641]{1,0:T(8,128)}, f32[1,1408]{1,0:T(1,128)}, f32[1,640]{1,0:T(1,128)}) custom-call(f32[736,640]{1,0:T(8,128)} %constant_dynamic-update-slice_fusion.12.g_ref, f32[2208,1408]{1,0:T(8,128)} %get-tuple-element.376.slope_ref, ...), custom_call_target="tpu_custom_call", output_to_operand_aliasing={{0}: (5, {}), {1}: (6, {})} | custom-call | flops 15456000000 | bytes 1000 | tf_op jit(solution)/shard_map/mlp_back/pallas_call | solution.py:669
  863.9 6.5 all-to-all-done.8
  870.4 12.4 analysis.11
  887.8 8.0 fusion
  895.8 8.1 fusion.2
  904.0 8.5 fusion.4
  918.0 7.2 fusion.8
  925.2 11.9 add_add_fusion
  937.1 19.3 %fusion.55 = f32[641,1408]{1,0:T(8,128)S(1)} fusion(f32[2208,641]{1,0:T(8,128)} %bitcast.151, f32[2208,1408]{1,0:T(8,128)} %get-tuple-element.407), kind=kOutput, calls=%fused_computation.162 | convolution fusion | flops 11956690944 | bytes 21706880 | tf_op jit(solution)/shard_map/tc,th->ch/dot_general | solution.py:1058
  956.5 22.8 %convolution_add_fusion = f32[641,1408]{1,0:T(8,128)} fusion(f32[641,1408]{1,0:T(8,128)S(1)} %fusion.55, f32[2208,641]{1,0:T(8,128)S(1)} %bitcast.114, f32[2208,1408]{1,0:T(8,128)} %get-tuple-element.408), kind=kOutput, calls=%fused_computation.22 | convolution fusion | flops 11957594112 | bytes 25316992 | tf_op jit(solution)/shard_map/tc,th->ch/dot_general | solution.py:1058
  979.3 12.0 filter_back.3
  991.3 26.7 %all-to-all-done.9 = f32[8,12,24,640]{3,2,1,0:T(8,128)} async-done(((f32[8,12,24,640]{3,2,1,0:T(8,128)}), f32[8,12,24,640]{3,2,1,0:T(8,128)}, u32[]{:S(2)}, u32[]{:S(2)}) %all-to-all-start.9) | async-done | bytes 5898272 | tf_op jit(solution)/shard_map/all_to_all | solution.py:879
  1034.7 12.0 filter_back.2
  1055.1 133.3 %scatter_sum.1 = (f32[96,1408]{1,0:T(8,128)}, f32[96,1408]{1,0:T(8,128)}) custom-call(f32[768,1408]{1,0:T(8,128)} %select_maximum_fusion.refs_0_, f32[768,1408]{1,0:T(8,128)} %pad.48.refs_1_), custom_call_target="tpu_custom_call" | custom-call | flops 80000000000 | bytes 1000 | tf_op jit(solution)/shard_map/scatter_sum/pallas_call | solution.py:391
  1193.1 46.1 %gather.1 = (f32[768,1408]{1,0:T(8,128)}, f32[768,1408]{1,0:T(8,128)}) custom-call(f32[96,1408]{1,0:T(8,128)} %get-tuple-element.440.refs_0_, f32[96,1408]{1,0:T(8,128)} %get-tuple-element.441.refs_1_), custom_call_target="tpu_custom_call" | custom-call | flops 40000000000 | bytes 1000 | tf_op jit(solution)/shard_map/gather/pallas_call | solution.py:413
  1255.4 11.0 maximum_multiply_fusion
  1266.3 19.7 %copy.93 = f32[2,12,180,641]{3,0,2,1:T(2,128)} copy(f32[2,12,180,641]{3,2,1,0:T(8,128)} %maximum_multiply_fusion) | data formatting | bytes 22152960
  1293.3 13.1 synthesis.10.refs_0_
  1306.4 17.3 %all-to-all-done.11.y_ref = f32[8,12,24,640]{3,2,1,0:T(8,128)} async-done(((f32[8,12,24,640]{3,2,1,0:T(8,128)}), f32[8,12,24,640]{3,2,1,0:T(8,128)}, u32[]{:S(2)}, u32[]{:S(2)}) %all-to-all-start.11) | async-done | bytes 5898272 | tf_op jit(solution)/shard_map/all_to_all | solution.py:879
  1323.7 16.5 %synthesis.11 = f32[12,180,2,633]{3,2,1,0:T(2,128)} custom-call(f32[8,12,24,640]{3,2,1,0:T(8,128)} %all-to-all-done.11.y_ref, bf16[184,192]{1,0:T(8,128)(2,1)} %constant.102.clone.th_ref, bf16[184,192]{1,0:T(8,128)(2,1)} %constant.103.clone.tl_ref, f32[12,184,641]{2,1,0:T(8,128)} %bitcast.135, f32[12,184,641]{2,1,0:T(8,128)} %synthesis.10.refs_0_), custom_call_target="tpu_custom_call" | custom-call | flops 14400000000 | bytes 1000 | tf_op jit(solution)/shard_map/synthesis/pallas_call | solution.py:250
  (343 shorter events, 261.6 us)
Async XLA Ops:
  21.7 137.0 %all-to-all-start = ((f32[8,12,24,640]{3,2,1,0:T(8,128)}), f32[8,12,24,640]{3,2,1,0:T(8,128)}, u32[]{:S(2)}, u32[]{:S(2)}) async-start(f32[8,12,24,640]{3,2,1,0:T(8,128)} %get-tuple-element.230), calls=%async_computation | async-start | bytes 11796480 | tf_op jit(solution)/shard_map/all_to_all | solution.py:879
  158.7 135.4 %all-to-all-start.1 = ((f32[8,12,24,640]{3,2,1,0:T(8,128)}), f32[8,12,24,640]{3,2,1,0:T(8,128)}, u32[]{:S(2)}, u32[]{:S(2)}) async-start(f32[8,12,24,640]{3,2,1,0:T(8,128)} %get-tuple-element.235), calls=%async_computation.1 | async-start | bytes 11796480 | tf_op jit(solution)/shard_map/all_to_all | solution.py:879
  294.1 135.6 %all-to-all-start.2 = ((f32[8,12,24,640]{3,2,1,0:T(8,128)}), f32[8,12,24,640]{3,2,1,0:T(8,128)}, u32[]{:S(2)}, u32[]{:S(2)}) async-start(f32[8,12,24,640]{3,2,1,0:T(8,128)} %bitcast.119), calls=%async_computation.2 | async-start | bytes 11796480 | tf_op jit(solution)/shard_map/all_to_all | solution.py:879
  429.7 56.0 %all-to-all-start.3 = ((f32[8,4,24,640]{3,2,1,0:T(8,128)}), f32[8,4,24,640]{3,2,1,0:T(8,128)S(1)}, u32[]{:S(2)}, u32[]{:S(2)}) async-start(f32[8,4,24,640]{3,2,1,0:T(8,128)} %bitcast.130), calls=%async_computation.3 | async-start | bytes 3932160 | tf_op jit(solution)/shard_map/all_to_all | solution.py:879
  482.2 34.3 %collective-permute-start = (f32[184,640]{1,0:T(8,128)}, f32[184,640]{1,0:T(8,128)}, u32[]{:S(2)}, u32[]{:S(2)}) collective-permute-start(f32[184,640]{1,0:T(8,128)} %get-tuple-element.489), channel_id=1, source_target_pairs={{0,8},{8,0},{16,24},{24,16},{1,9},{9,1},{17,25},{25,17},{2,10},{10... | collective-permute-start | bytes 1413128 | tf_op jit(solution)/shard_map/ppermute | solution.py:886
  483.8 33.3 %collective-permute-start.1 = (f32[184,640]{1,0:T(8,128)}, f32[184,640]{1,0:T(8,128)}, u32[]{:S(2)}, u32[]{:S(2)}) collective-permute-start(f32[184,640]{1,0:T(8,128)} %get-tuple-element.488), channel_id=1, source_target_pairs={{0,16},{8,24},{16,0},{24,8},{1,17},{9,25},{17,1},{25,9},{2,18},{10... | collective-permute-start | bytes 1413128 | tf_op jit(solution)/shard_map/ppermute | solution.py:886
  485.3 32.4 %collective-permute-start.2 = (f32[184,640]{1,0:T(8,128)}, f32[184,640]{1,0:T(8,128)}, u32[]{:S(2)}, u32[]{:S(2)}) collective-permute-start(f32[184,640]{1,0:T(8,128)} %get-tuple-element.487), channel_id=1, source_target_pairs={{0,24},{8,16},{16,8},{24,0},{1,25},{9,17},{17,9},{25,1},{2,26},{10... | collective-permute-start | bytes 1413128 | tf_op jit(solution)/shard_map/ppermute | solution.py:886
  487.0 58.0 %all-to-all-start.4 = ((f32[8,4,24,640]{3,2,1,0:T(8,128)}), f32[8,4,24,640]{3,2,1,0:T(8,128)S(1)}, u32[]{:S(2)}, u32[]{:S(2)}) async-start(f32[8,4,24,640]{3,2,1,0:T(8,128)} %bitcast.128), calls=%async_computation.4 | async-start | bytes 3932160 | tf_op jit(solution)/shard_map/all_to_all | solution.py:879
  512.3 48.0 %collective-permute-start.6 = (f32[184,640]{1,0:T(8,128)S(1)}, f32[184,640]{1,0:T(8,128)}, u32[]{:S(2)}, u32[]{:S(2)}) collective-permute-start(f32[184,640]{1,0:T(8,128)S(1)} %get-tuple-element.481), channel_id=1, source_target_pairs={{0,8},{8,0},{16,24},{24,16},{1,9},{9,1},{17,25},{25,17},{2,10},{10... | collective-permute-start | bytes 1413128 | tf_op jit(solution)/shard_map/ppermute | solution.py:886
  513.7 64.2 %collective-permute-start.7 = (f32[184,640]{1,0:T(8,128)S(1)}, f32[184,640]{1,0:T(8,128)}, u32[]{:S(2)}, u32[]{:S(2)}) collective-permute-start(f32[184,640]{1,0:T(8,128)S(1)} %get-tuple-element.480), channel_id=1, source_target_pairs={{0,16},{8,24},{16,0},{24,8},{1,17},{9,25},{17,1},{25,9},{2,18},{10... | collective-permute-start | bytes 1413128 | tf_op jit(solution)/shard_map/ppermute | solution.py:886
  516.5 35.0 %collective-permute-start.9 = (f32[184,640]{1,0:T(8,128)}, f32[184,640]{1,0:T(8,128)}, u32[]{:S(2)}, u32[]{:S(2)}) collective-permute-start(f32[184,640]{1,0:T(8,128)} %get-tuple-element.477), channel_id=1, source_target_pairs={{0,8},{8,0},{16,24},{24,16},{1,9},{9,1},{17,25},{25,17},{2,10},{10... | collective-permute-start | bytes 1413128 | tf_op jit(solution)/shard_map/ppermute | solution.py:886
  517.1 35.1 %collective-permute-start.10 = (f32[184,640]{1,0:T(8,128)}, f32[184,640]{1,0:T(8,128)}, u32[]{:S(2)}, u32[]{:S(2)}) collective-permute-start(f32[184,640]{1,0:T(8,128)} %get-tuple-element.476), channel_id=1, source_target_pairs={{0,16},{8,24},{16,0},{24,8},{1,17},{9,25},{17,1},{25,9},{2,18},{10... | collective-permute-start | bytes 1413128 | tf_op jit(solution)/shard_map/ppermute | solution.py:886
  517.6 36.0 %collective-permute-start.11 = (f32[184,640]{1,0:T(8,128)}, f32[184,640]{1,0:T(8,128)}, u32[]{:S(2)}, u32[]{:S(2)}) collective-permute-start(f32[184,640]{1,0:T(8,128)} %get-tuple-element.475), channel_id=1, source_target_pairs={{0,24},{8,16},{16,8},{24,0},{1,25},{9,17},{17,9},{25,1},{2,26},{10... | collective-permute-start | bytes 1413128 | tf_op jit(solution)/shard_map/ppermute | solution.py:886
  546.3 95.5 %all-to-all-start.5 = ((f32[8,4,24,640]{3,2,1,0:T(8,128)}), f32[8,4,24,640]{3,2,1,0:T(8,128)S(1)}, u32[]{:S(2)}, u32[]{:S(2)}) async-start(f32[8,4,24,640]{3,2,1,0:T(8,128)} %bitcast.126), calls=%async_computation.5 | async-start | bytes 3932160 | tf_op jit(solution)/shard_map/all_to_all | solution.py:879
  551.6 26.4 %collective-permute-start.8 = (f32[184,640]{1,0:T(8,128)S(1)}, f32[184,640]{1,0:T(8,128)S(1)}, u32[]{:S(2)}, u32[]{:S(2)}) collective-permute-start(f32[184,640]{1,0:T(8,128)S(1)} %get-tuple-element.479), channel_id=1, source_target_pairs={{0,24},{8,16},{16,8},{24,0},{1,25},{9,17},{17,9},{25,1},{2,26},{10... | collective-permute-start | bytes 1413128 | tf_op jit(solution)/shard_map/ppermute | solution.py:886
  552.1 25.9 %collective-permute-start.3 = (f32[184,640]{1,0:T(8,128)}, f32[184,640]{1,0:T(8,128)S(1)}, u32[]{:S(2)}, u32[]{:S(2)}) collective-permute-start(f32[184,640]{1,0:T(8,128)} %get-tuple-element.485), channel_id=1, source_target_pairs={{0,8},{8,0},{16,24},{24,16},{1,9},{9,1},{17,25},{25,17},{2,10},{10... | collective-permute-start | bytes 1413128 | tf_op jit(solution)/shard_map/ppermute | solution.py:886
  553.6 24.4 %collective-permute-start.4 = (f32[184,640]{1,0:T(8,128)}, f32[184,640]{1,0:T(8,128)S(1)}, u32[]{:S(2)}, u32[]{:S(2)}) collective-permute-start(f32[184,640]{1,0:T(8,128)} %get-tuple-element.484), channel_id=1, source_target_pairs={{0,16},{8,24},{16,0},{24,8},{1,17},{9,25},{17,1},{25,9},{2,18},{10... | collective-permute-start | bytes 1413128 | tf_op jit(solution)/shard_map/ppermute | solution.py:886
  560.3 25.7 %collective-permute-start.5 = (f32[184,640]{1,0:T(8,128)S(1)}, f32[184,640]{1,0:T(8,128)S(1)}, u32[]{:S(2)}, u32[]{:S(2)}) collective-permute-start(f32[184,640]{1,0:T(8,128)S(1)} %copy-done.17), channel_id=1, source_target_pairs={{0,24},{8,16},{16,8},{24,0},{1,25},{9,17},{17,9},{25,1},{2,26},{10... | collective-permute-start | bytes 1413128 | tf_op jit(solution)/shard_map/ppermute | solution.py:886
  588.5 13.7 %collective-permute-start.15 = (f32[184,640]{1,0:T(8,128)S(1)}, f32[184,640]{1,0:T(8,128)S(1)}, u32[]{:S(2)}, u32[]{:S(2)}) collective-permute-start(f32[184,640]{1,0:T(8,128)S(1)} %get-tuple-element.473), channel_id=1, source_target_pairs={{0,8},{8,0},{16,24},{24,16},{1,9},{9,1},{17,25},{25,17},{2,10},{10... | collective-permute-start | bytes 1413128 | tf_op jit(solution)/shard_map/ppermute | solution.py:886
  589.0 21.5 %collective-permute-start.16 = (f32[184,640]{1,0:T(8,128)S(1)}, f32[184,640]{1,0:T(8,128)S(1)}, u32[]{:S(2)}, u32[]{:S(2)}) collective-permute-start(f32[184,640]{1,0:T(8,128)S(1)} %get-tuple-element.472), channel_id=1, source_target_pairs={{0,16},{8,24},{16,0},{24,8},{1,17},{9,25},{17,1},{25,9},{2,18},{10... | collective-permute-start | bytes 1413128 | tf_op jit(solution)/shard_map/ppermute | solution.py:886
  589.6 22.7 %collective-permute-start.17 = (f32[184,640]{1,0:T(8,128)S(1)}, f32[184,640]{1,0:T(8,128)S(1)}, u32[]{:S(2)}, u32[]{:S(2)}) collective-permute-start(f32[184,640]{1,0:T(8,128)S(1)} %get-tuple-element.471), channel_id=1, source_target_pairs={{0,24},{8,16},{16,8},{24,0},{1,25},{9,17},{17,9},{25,1},{2,26},{10... | collective-permute-start | bytes 1413128 | tf_op jit(solution)/shard_map/ppermute | solution.py:886
  600.7 21.7 %collective-permute-start.12 = (f32[184,640]{1,0:T(8,128)}, f32[184,640]{1,0:T(8,128)S(1)}, u32[]{:S(2)}, u32[]{:S(2)}) collective-permute-start(f32[184,640]{1,0:T(8,128)} %get-tuple-element.294), channel_id=1, source_target_pairs={{0,8},{8,0},{16,24},{24,16},{1,9},{9,1},{17,25},{25,17},{2,10},{10... | collective-permute-start | bytes 1413128 | tf_op jit(solution)/shard_map/ppermute | solution.py:886
  601.4 30.1 %collective-permute-start.13 = (f32[184,640]{1,0:T(8,128)}, f32[184,640]{1,0:T(8,128)S(1)}, u32[]{:S(2)}, u32[]{:S(2)}) collective-permute-start(f32[184,640]{1,0:T(8,128)} %get-tuple-element.295), channel_id=1, source_target_pairs={{0,16},{8,24},{16,0},{24,8},{1,17},{9,25},{17,1},{25,9},{2,18},{10... | collective-permute-start | bytes 1413128 | tf_op jit(solution)/shard_map/ppermute | solution.py:886
  602.2 30.1 %collective-permute-start.14 = (f32[184,640]{1,0:T(8,128)}, f32[184,640]{1,0:T(8,128)S(1)}, u32[]{:S(2)}, u32[]{:S(2)}) collective-permute-start(f32[184,640]{1,0:T(8,128)} %get-tuple-element.296), channel_id=1, source_target_pairs={{0,24},{8,16},{16,8},{24,0},{1,25},{9,17},{17,9},{25,1},{2,26},{10... | collective-permute-start | bytes 1413128 | tf_op jit(solution)/shard_map/ppermute | solution.py:886
  668.7 29.9 %collective-permute-start.21 = (f32[184,640]{1,0:T(8,128)}, f32[184,640]{1,0:T(8,128)}, u32[]{:S(2)}, u32[]{:S(2)}) collective-permute-start(f32[184,640]{1,0:T(8,128)} %get-tuple-element.329), channel_id=1, source_target_pairs={{0,8},{8,0},{16,24},{24,16},{1,9},{9,1},{17,25},{25,17},{2,10},{10... | collective-permute-start | bytes 1413128 | tf_op jit(solution)/shard_map/ppermute | solution.py:886
  670.3 29.4 %collective-permute-start.22 = (f32[184,640]{1,0:T(8,128)}, f32[184,640]{1,0:T(8,128)}, u32[]{:S(2)}, u32[]{:S(2)}) collective-permute-start(f32[184,640]{1,0:T(8,128)} %get-tuple-element.330), channel_id=1, source_target_pairs={{0,16},{8,24},{16,0},{24,8},{1,17},{9,25},{17,1},{25,9},{2,18},{10... | collective-permute-start | bytes 1413128 | tf_op jit(solution)/shard_map/ppermute | solution.py:886
  671.0 29.7 %collective-permute-start.23 = (f32[184,640]{1,0:T(8,128)}, f32[184,640]{1,0:T(8,128)}, u32[]{:S(2)}, u32[]{:S(2)}) collective-permute-start(f32[184,640]{1,0:T(8,128)} %get-tuple-element.331), channel_id=1, source_target_pairs={{0,24},{8,16},{16,8},{24,0},{1,25},{9,17},{17,9},{25,1},{2,26},{10... | collective-permute-start | bytes 1413128 | tf_op jit(solution)/shard_map/ppermute | solution.py:886
  672.2 70.3 %all-to-all-start.6 = ((f32[8,4,24,640]{3,2,1,0:T(8,128)}), f32[8,4,24,640]{3,2,1,0:T(8,128)S(1)}, u32[]{:S(2)}, u32[]{:S(2)}) async-start(f32[8,4,24,640]{3,2,1,0:T(8,128)} %analysis.8), calls=%async_computation.6 | async-start | bytes 3932160 | tf_op jit(solution)/shard_map/all_to_all | solution.py:879
  696.1 51.7 %collective-permute-start.18 = (f32[184,640]{1,0:T(8,128)S(1)}, f32[184,640]{1,0:T(8,128)}, u32[]{:S(2)}, u32[]{:S(2)}) collective-permute-start(f32[184,640]{1,0:T(8,128)S(1)} %get-tuple-element.469), channel_id=1, source_target_pairs={{0,8},{8,0},{16,24},{24,16},{1,9},{9,1},{17,25},{25,17},{2,10},{10... | collective-permute-start | bytes 1413128 | tf_op jit(solution)/shard_map/ppermute | solution.py:886
  697.7 50.2 %collective-permute-start.19 = (f32[184,640]{1,0:T(8,128)S(1)}, f32[184,640]{1,0:T(8,128)}, u32[]{:S(2)}, u32[]{:S(2)}) collective-permute-start(f32[184,640]{1,0:T(8,128)S(1)} %get-tuple-element.468), channel_id=1, source_target_pairs={{0,16},{8,24},{16,0},{24,8},{1,17},{9,25},{17,1},{25,9},{2,18},{10... | collective-permute-start | bytes 1413128 | tf_op jit(solution)/shard_map/ppermute | solution.py:886
  701.8 21.8 %collective-permute-start.33 = (f32[184,640]{1,0:T(8,128)}, f32[184,640]{1,0:T(8,128)S(1)}, u32[]{:S(2)}, u32[]{:S(2)}) collective-permute-start(f32[184,640]{1,0:T(8,128)} %get-tuple-element.372), channel_id=1, source_target_pairs={{0,8},{8,0},{16,24},{24,16},{1,9},{9,1},{17,25},{25,17},{2,10},{10... | collective-permute-start | bytes 1413128 | tf_op jit(solution)/shard_map/ppermute | solution.py:886
  702.3 38.6 %collective-permute-start.34 = (f32[184,640]{1,0:T(8,128)S(1)}, f32[184,640]{1,0:T(8,128)S(1)}, u32[]{:S(2)}, u32[]{:S(2)}) collective-permute-start(f32[184,640]{1,0:T(8,128)S(1)} %copy-done.52), channel_id=1, source_target_pairs={{0,16},{8,24},{16,0},{24,8},{1,17},{9,25},{17,1},{25,9},{2,18},{10... | collective-permute-start | bytes 1413128 | tf_op jit(solution)/shard_map/ppermute | solution.py:886
  703.6 38.1 %collective-permute-start.35 = (f32[184,640]{1,0:T(8,128)S(1)}, f32[184,640]{1,0:T(8,128)S(1)}, u32[]{:S(2)}, u32[]{:S(2)}) collective-permute-start(f32[184,640]{1,0:T(8,128)S(1)} %copy-done.51), channel_id=1, source_target_pairs={{0,24},{8,16},{16,8},{24,0},{1,25},{9,17},{17,9},{25,1},{2,26},{10... | collective-permute-start | bytes 1413128 | tf_op jit(solution)/shard_map/ppermute | solution.py:886
  723.7 24.2 %collective-permute-start.20 = (f32[184,640]{1,0:T(8,128)S(1)}, f32[184,640]{1,0:T(8,128)}, u32[]{:S(2)}, u32[]{:S(2)}) collective-permute-start(f32[184,640]{1,0:T(8,128)S(1)} %get-tuple-element.467), channel_id=1, source_target_pairs={{0,24},{8,16},{16,8},{24,0},{1,25},{9,17},{17,9},{25,1},{2,26},{10... | collective-permute-start | bytes 1413128 | tf_op jit(solution)/shard_map/ppermute | solution.py:886
  756.5 25.2 %collective-permute-start.24 = (f32[184,640]{1,0:T(8,128)}, f32[184,640]{1,0:T(8,128)S(1)}, u32[]{:S(2)}, u32[]{:S(2)}) collective-permute-start(f32[184,640]{1,0:T(8,128)} %get-tuple-element.349), channel_id=1, source_target_pairs={{0,8},{8,0},{16,24},{24,16},{1,9},{9,1},{17,25},{25,17},{2,10},{10... | collective-permute-start | bytes 1413128 | tf_op jit(solution)/shard_map/ppermute | solution.py:886
  756.6 25.1 %collective-permute-start.25 = (f32[184,640]{1,0:T(8,128)}, f32[184,640]{1,0:T(8,128)S(1)}, u32[]{:S(2)}, u32[]{:S(2)}) collective-permute-start(f32[184,640]{1,0:T(8,128)} %get-tuple-element.351), channel_id=1, source_target_pairs={{0,16},{8,24},{16,0},{24,8},{1,17},{9,25},{17,1},{25,9},{2,18},{10... | collective-permute-start | bytes 1413128 | tf_op jit(solution)/shard_map/ppermute | solution.py:886
  757.6 24.1 %collective-permute-start.26 = (f32[184,640]{1,0:T(8,128)}, f32[184,640]{1,0:T(8,128)S(1)}, u32[]{:S(2)}, u32[]{:S(2)}) collective-permute-start(f32[184,640]{1,0:T(8,128)} %get-tuple-element.353), channel_id=1, source_target_pairs={{0,24},{8,16},{16,8},{24,0},{1,25},{9,17},{17,9},{25,1},{2,26},{10... | collective-permute-start | bytes 1413128 | tf_op jit(solution)/shard_map/ppermute | solution.py:886
  760.1 53.5 %all-to-all-start.7 = ((f32[8,4,24,640]{3,2,1,0:T(8,128)}), f32[8,4,24,640]{3,2,1,0:T(8,128)S(1)}, u32[]{:S(2)}, u32[]{:S(2)}) async-start(f32[8,4,24,640]{3,2,1,0:T(8,128)} %analysis.9), calls=%async_computation.7 | async-start | bytes 3932160 | tf_op jit(solution)/shard_map/all_to_all | solution.py:879
  782.5 25.2 %collective-permute-start.27 = (f32[184,640]{1,0:T(8,128)S(1)}, f32[184,640]{1,0:T(8,128)S(1)}, u32[]{:S(2)}, u32[]{:S(2)}) collective-permute-start(f32[184,640]{1,0:T(8,128)S(1)} %copy-done.50), channel_id=1, source_target_pairs={{0,8},{8,0},{16,24},{24,16},{1,9},{9,1},{17,25},{25,17},{2,10},{10... | collective-permute-start | bytes 1413128 | tf_op jit(solution)/shard_map/ppermute | solution.py:886
  782.6 25.1 %collective-permute-start.28 = (f32[184,640]{1,0:T(8,128)S(1)}, f32[184,640]{1,0:T(8,128)S(1)}, u32[]{:S(2)}, u32[]{:S(2)}) collective-permute-start(f32[184,640]{1,0:T(8,128)S(1)} %copy-done.49), channel_id=1, source_target_pairs={{0,16},{8,24},{16,0},{24,8},{1,17},{9,25},{17,1},{25,9},{2,18},{10... | collective-permute-start | bytes 1413128 | tf_op jit(solution)/shard_map/ppermute | solution.py:886
  783.6 24.2 %collective-permute-start.29 = (f32[184,640]{1,0:T(8,128)S(1)}, f32[184,640]{1,0:T(8,128)S(1)}, u32[]{:S(2)}, u32[]{:S(2)}) collective-permute-start(f32[184,640]{1,0:T(8,128)S(1)} %copy-done.48), channel_id=1, source_target_pairs={{0,24},{8,16},{16,8},{24,0},{1,25},{9,17},{17,9},{25,1},{2,26},{10... | collective-permute-start | bytes 1413128 | tf_op jit(solution)/shard_map/ppermute | solution.py:886
  807.7 18.1 %collective-permute-start.30 = (f32[184,640]{1,0:T(8,128)}, f32[184,640]{1,0:T(8,128)}, u32[]{:S(2)}, u32[]{:S(2)}) collective-permute-start(f32[184,640]{1,0:T(8,128)} %get-tuple-element.364), channel_id=1, source_target_pairs={{0,8},{8,0},{16,24},{24,16},{1,9},{9,1},{17,25},{25,17},{2,10},{10... | collective-permute-start | bytes 1413128 | tf_op jit(solution)/shard_map/ppermute | solution.py:886
  807.9 19.8 %collective-permute-start.31 = (f32[184,640]{1,0:T(8,128)}, f32[184,640]{1,0:T(8,128)}, u32[]{:S(2)}, u32[]{:S(2)}) collective-permute-start(f32[184,640]{1,0:T(8,128)} %get-tuple-element.365), channel_id=1, source_target_pairs={{0,16},{8,24},{16,0},{24,8},{1,17},{9,25},{17,1},{25,9},{2,18},{10... | collective-permute-start | bytes 1413128 | tf_op jit(solution)/shard_map/ppermute | solution.py:886
  808.9 22.0 %collective-permute-start.32 = (f32[184,640]{1,0:T(8,128)}, f32[184,640]{1,0:T(8,128)S(1)}, u32[]{:S(2)}, u32[]{:S(2)}) collective-permute-start(f32[184,640]{1,0:T(8,128)} %get-tuple-element.366), channel_id=1, source_target_pairs={{0,24},{8,16},{16,8},{24,0},{1,25},{9,17},{17,9},{25,1},{2,26},{10... | collective-permute-start | bytes 1413128 | tf_op jit(solution)/shard_map/ppermute | solution.py:886
  818.9 51.5 %all-to-all-start.8 = ((f32[8,4,24,640]{3,2,1,0:T(8,128)}), f32[8,4,24,640]{3,2,1,0:T(8,128)S(1)}, u32[]{:S(2)}, u32[]{:S(2)}) async-start(f32[8,4,24,640]{3,2,1,0:T(8,128)} %analysis.10), calls=%async_computation.8 | async-start | bytes 3932160 | tf_op jit(solution)/shard_map/all_to_all | solution.py:879
  882.8 135.2 %all-to-all-start.9 = ((f32[8,12,24,640]{3,2,1,0:T(8,128)}), f32[8,12,24,640]{3,2,1,0:T(8,128)}, u32[]{:S(2)}, u32[]{:S(2)}) async-start(f32[8,12,24,640]{3,2,1,0:T(8,128)} %analysis.11), calls=%async_computation.9 | async-start | bytes 11796480 | tf_op jit(solution)/shard_map/all_to_all | solution.py:879
  1018.2 170.2 %all-to-all-start.10 = ((f32[8,12,24,640]{3,2,1,0:T(8,128)}), f32[8,12,24,640]{3,2,1,0:T(8,128)}, u32[]{:S(2)}, u32[]{:S(2)}) async-start(f32[8,12,24,640]{3,2,1,0:T(8,128)} %bitcast.120), calls=%async_computation.10 | async-start | bytes 11796480 | tf_op jit(solution)/shard_map/all_to_all | solution.py:879
  1188.4 135.3 %all-to-all-start.11 = ((f32[8,12,24,640]{3,2,1,0:T(8,128)}), f32[8,12,24,640]{3,2,1,0:T(8,128)}, u32[]{:S(2)}, u32[]{:S(2)}) async-start(f32[8,12,24,640]{3,2,1,0:T(8,128)} %bitcast.121), calls=%async_computation.11 | async-start | bytes 11796480 | tf_op jit(solution)/shard_map/all_to_all | solution.py:879
  (68 other events, 654.7 us)

commit v2 on v1

--- a/solution.py
+++ b/solution.py
@@ -946,8 +946,7 @@
         out, part = crps(fields, own, observed_share[q], area_share[q], places, channels)
         losses.append(part)
         results[q] = out
-        if q != 1:
-            got[0, q] = returned(0, q)
+        got[0, q] = returned(0, q)
         return out[0]
 
     def returned(b, q):
@@ -987,32 +986,32 @@
         return f
 
     token = ()
+    in_turns = len(groups) == 3
     for b in range(final):
         mix(b, 0, *token)
         for q in every:
+            if in_turns and b == final - 1 and q == 2:
+                break
             token = (forward(b, q, *token),)
-            if b == final - 1 and q == 1:
-                synths[final].append(to_owner(tie(h[1], *token)))
-    ready = lambda q: [shares[b, q] for b in range(final)]
-    if len(groups) == 3:
-        for q in (0, 1):
-            mix(final, q, ready(q), *token)
-            token = (forward(final, q),)
-            if q == 0:
-                synths[final].append(to_owner(tie(h[2], *token)))
-        token = (score(0, ready(2), *token),)
+    if in_turns:
+        synths[final].append(to_owner(tie(h[1], *token)))
+        mix(final, 0, *token)
+        token = (forward(final, 0),)
+        synths[final].append(to_owner(tie(h[2], *token)))
+        token = (forward(final - 1, 2, *token),)
+        token = (score(0, *token),)
+        mix(final, 1, *token)
+        token = (forward(final, 1),)
+        backward(0, 0, *token)
+        token = (send_back(0, [0]),)
         token = (score(1, *token),)
-        first_back = backward(0, 0, synths[final][2], *token)
-        results[1] = tie(results[1], first_back)
-        got[0, 1] = returned(0, 1)
-        for b in range(1, own):
-            results[0] = tie(results[0], got[0, 1])
-            got[b, 0] = returned(b, 0)
-        token = (send_back(0, [0]),)
         mix(final, 2, *token)
         token = (forward(final, 2),)
         backward(0, 1, *token)
         token = (send_back(0, [1]),)
+        for b in range(1, own):
+            results[0] = tie(results[0], *token)
+            got[b, 0] = returned(b, 0)
         token = (score(2, *token),)
         for b in range(1, own):
             token = (backward(b, 0, *token),)
@@ -1034,7 +1033,7 @@
             token = (score(q, *token),)
         for b in range(own):
             for q in every:
-                if b > 0 or q == 1:
+                if b > 0:
                     got[b, q] = returned(b, q)
                 token = (backward(b, q, *token),)
             token = (send_back(b, list(every)),)

time: 1350 us -> 1370 us (1.015)
  waiting for transfers between devices: 406 us -> 426 us
    ppermute x36, waiting for transfers between devices: 47.8 us -> 68 us  [swap(): return lax.ppermute(x, 'member', pairs)]
  transfers between devices with their start and end apart: 48 -> 48, of which waited for: 14 -> 19; matrix products, arithmetic and copies ran while one was open for 17% -> 17% of each run, Pallas kernels for 37% -> 40%
where the time goes in v2:
time: 1370 us; the launch traced here: 1360 us
  Pallas kernels  581 us (42%)
  waiting for transfers between devices  426 us (31%)
  local copies, waits for them, and re-layouts  117 us (9%)
  starting transfers between devices  106 us (8%)
  matrix products  94.2 us (7%)
  other arithmetic  28.8 us (2%)
    all_to_all x12, waiting for transfers between devices, to_owner(): lax.all_to_all(x, 'lat', split_axis=0, concat_axis=0, tiled=True)  358 us
    pallas_call x1, Pallas kernels, scatter_sum(): pl.pallas_call(functools.partial(scatter_sum_kernel, chains, near, len(xs...  133 us
    pallas_call x6, Pallas kernels, mlp(): pl.pallas_call(functools.partial(mlp_kernel, main), grid=(tokens // tile,...  103 us
    pallas_call x6, Pallas kernels, mlp_back(): pl.pallas_call(functools.partial(mlp_back_kernel, main), grid=(tokens //...  97.2 us
    ppermute x36, waiting for transfers between devices, swap(): return lax.ppermute(x, 'member', pairs)  68 us
    all_to_all x12, starting transfers between devices, to_owner(): lax.all_to_all(x, 'lat', split_axis=0, concat_axis=0, tiled=True)  59.1 us
    pallas_call x6, Pallas kernels, synthesis(): pl.pallas_call(functools.partial(synthesis_kernel, (devices, rows, main),...  57.9 us
    pallas_call x6, Pallas kernels, analysis(): pl.pallas_call(kernel, grid=(row_count,), in_specs=x_specs + [whole((tota...  57.6 us
  transfers between devices with their start and end apart: 48, of which 19 were waited for; matrix products, arithmetic and copies ran while one was open for 17% of the time, Pallas kernels for 40%

profile of v2, /device:TPU:0, one launch (start us, length us, event | category | flops | bytes accessed | tf_op | source)
XLA Modules:
  0.0 1359.2 jit_solution(11712741568934082032)
XLA Ops:
  6.5 15.2 %analysis.6 = (f32[12,184,641]{2,1,0:T(8,128)}, f32[8,12,24,640]{3,2,1,0:T(8,128)}) custom-call(f32[12,180,2,633]{3,2,1,0:T(2,128)} %bitcast.141, f32[2,12,184,256]{3,2,1,0:T(8,128)} %pad.40.noise_ref, bf16[192,184]{1,0:T(8,128)(2,1)} %constant.96.clone.refs_0_, bf16[192,184]{1,0:T(8,128)(2,1)} %constant.97.clone.refs_1_), custom_call_target="tpu_custom_call" | custom-call | flops 14400000000 | bytes 1000 | tf_op jit(solution)/shard_map/analysis/pallas_call | solution.py:191
  28.0 15.2 %analysis.7 = (f32[12,184,641]{2,1,0:T(8,128)}, f32[8,12,24,640]{3,2,1,0:T(8,128)}) custom-call(f32[12,180,2,633]{3,2,1,0:T(2,128)} %bitcast.142, f32[2,12,184,256]{3,2,1,0:T(8,128)} %pad.40.noise_ref, bf16[192,184]{1,0:T(8,128)(2,1)} %constant.96.clone.refs_0_, bf16[192,184]{1,0:T(8,128)(2,1)} %constant.97.clone.refs_1_), custom_call_target="tpu_custom_call" | custom-call | flops 14400000000 | bytes 1000 | tf_op jit(solution)/shard_map/analysis/pallas_call | solution.py:191
  43.2 115.4 %all-to-all-done = f32[8,12,24,640]{3,2,1,0:T(8,128)} async-done(((f32[8,12,24,640]{3,2,1,0:T(8,128)}), f32[8,12,24,640]{3,2,1,0:T(8,128)}, u32[]{:S(2)}, u32[]{:S(2)}) %all-to-all-start) | async-done | bytes 5898272 | tf_op jit(solution)/shard_map/all_to_all | solution.py:879
  168.5 11.9 filter.2
  180.4 113.7 %all-to-all-done.1 = f32[8,12,24,640]{3,2,1,0:T(8,128)} async-done(((f32[8,12,24,640]{3,2,1,0:T(8,128)}), f32[8,12,24,640]{3,2,1,0:T(8,128)}, u32[]{:S(2)}, u32[]{:S(2)}) %all-to-all-start.1) | async-done | bytes 5898272 | tf_op jit(solution)/shard_map/all_to_all | solution.py:879
  300.5 6.7 pad_slice_fusion
  326.8 11.9 weights.1
  338.7 11.8 filter.3
  350.5 78.9 %all-to-all-done.2.y_ref = f32[8,12,24,640]{3,2,1,0:T(8,128)} async-done(((f32[8,12,24,640]{3,2,1,0:T(8,128)}), f32[8,12,24,640]{3,2,1,0:T(8,128)}, u32[]{:S(2)}, u32[]{:S(2)}) %all-to-all-start.2) | async-done | bytes 5898272 | tf_op jit(solution)/shard_map/all_to_all | solution.py:879
  433.3 13.0 synthesis.6
  446.4 17.2 %mlp.6 = (f32[2208,1408]{1,0:T(8,128)}, f32[2208,1408]{1,0:T(8,128)}, f32[2208,641]{1,0:T(8,128)}, f32[736,640]{1,0:T(8,128)}) custom-call(f32[2208,641]{1,0:T(8,128)} %bitcast.145, bf16[3,640,1408]{2,1,0:T(8,128)(2,1)} %get-tuple-element.241.w1, f32[1,1408]{1,0:T(1,128)} %get-tuple-element.293.w1e, f32[1,1408]{1,0:T(1,128)} %pad.42.b1, ...), custom_call_target="tpu_custom_call" | custom-call | flops 16928000000 | bytes 1000 | tf_op jit(solution)/shard_map/mlp/pallas_call | solution.py:617
  469.4 17.2 %mlp.7 = (f32[2208,1408]{1,0:T(8,128)}, f32[2208,1408]{1,0:T(8,128)}, f32[2208,641]{1,0:T(8,128)}, f32[736,640]{1,0:T(8,128)}) custom-call(f32[2208,641]{1,0:T(8,128)} %bitcast.146, bf16[3,640,1408]{2,1,0:T(8,128)(2,1)} %get-tuple-element.241.w1, f32[1,1408]{1,0:T(1,128)} %get-tuple-element.293.w1e, ...), custom_call_target="tpu_custom_call", output_to_operand_aliasing={{0}: (8, {}), {1}: (9, {}), {2}: (10, {})} | custom-call | flops 16928000000 | bytes 1000 | tf_op jit(solution)/shard_map/mlp/pallas_call | solution.py:617
  498.5 17.1 %mlp.8 = (f32[2208,1408]{1,0:T(8,128)}, f32[2208,1408]{1,0:T(8,128)}, f32[2208,641]{1,0:T(8,128)}, f32[736,640]{1,0:T(8,128)}) custom-call(f32[2208,641]{1,0:T(8,128)} %bitcast.109, bf16[3,640,1408]{2,1,0:T(8,128)(2,1)} %get-tuple-element.241.w1, f32[1,1408]{1,0:T(1,128)} %get-tuple-element.293.w1e, f32[1,1408]{1,0:T(1,128)} %pad.42.b1, ...), custom_call_target="tpu_custom_call" | custom-call | flops 16928000000 | bytes 1000 | tf_op jit(solution)/shard_map/mlp/pallas_call | solution.py:617
  521.5 17.2 %mlp.9 = (f32[2208,1408]{1,0:T(8,128)}, f32[2208,1408]{1,0:T(8,128)}, f32[2208,641]{1,0:T(8,128)}, f32[736,640]{1,0:T(8,128)}) custom-call(f32[2208,641]{1,0:T(8,128)} %bitcast.147, bf16[3,640,1408]{2,1,0:T(8,128)(2,1)} %get-tuple-element.241.w1, f32[1,1408]{1,0:T(1,128)} %get-tuple-element.293.w1e, ...), custom_call_target="tpu_custom_call", output_to_operand_aliasing={{0}: (8, {}), {1}: (9, {}), {2}: (10, {})} | custom-call | flops 16928000000 | bytes 1000 | tf_op jit(solution)/shard_map/mlp/pallas_call | solution.py:617
  543.4 8.8 crps.3
  568.7 17.2 %collective-permute-done.13 = f32[184,640]{1,0:T(8,128)S(1)} collective-permute-done((f32[184,640]{1,0:T(8,128)}, f32[184,640]{1,0:T(8,128)S(1)}, u32[]{:S(2)}, u32[]{:S(2)}) %collective-permute-start.13) | collective-permute-done | bytes 471072 | tf_op jit(solution)/shard_map/ppermute | solution.py:886
  593.9 17.3 %mlp.10 = (f32[2208,1408]{1,0:T(8,128)}, f32[2208,1408]{1,0:T(8,128)}, f32[2208,641]{1,0:T(8,128)}, f32[736,640]{1,0:T(8,128)}) custom-call(f32[2208,641]{1,0:T(8,128)} %bitcast.110, bf16[3,640,1408]{2,1,0:T(8,128)(2,1)} %get-tuple-element.241.w1, f32[1,1408]{1,0:T(1,128)} %get-tuple-element.293.w1e, ...), custom_call_target="tpu_custom_call", output_to_operand_aliasing={{0}: (8, {}), {1}: (9, {}), {2}: (10, {})} | custom-call | flops 16928000000 | bytes 1000 | tf_op jit(solution)/shard_map/mlp/pallas_call | solution.py:617
  621.8 16.1 %mlp_back.6 = (f32[2208,1408]{1,0:T(8,128)}, f32[2208,641]{1,0:T(8,128)}, f32[1,1408]{1,0:T(1,128)}, f32[1,640]{1,0:T(1,128)}) custom-call(f32[736,640]{1,0:T(8,128)} %constant_dynamic-update-slice_fusion.20.g_ref, f32[2208,1408]{1,0:T(8,128)} %get-tuple-element.290.slope_ref, bf16[3,640,1408]{2,1,0:T(8,128)(2,1)} %get-tuple-element.291.w2, ...), custom_call_target="tpu_custom_call" | custom-call | flops 15456000000 | bytes 1000 | tf_op jit(solution)/shard_map/mlp_back/pallas_call | solution.py:669
  643.7 8.8 crps.4
  670.4 7.9 collective-permute-done.22
  690.4 17.1 %mlp.11 = (f32[2208,1408]{1,0:T(8,128)}, f32[2208,1408]{1,0:T(8,128)}, f32[2208,641]{1,0:T(8,128)}, f32[736,640]{1,0:T(8,128)}) custom-call(f32[2208,641]{1,0:T(8,128)} %bitcast.111, bf16[3,640,1408]{2,1,0:T(8,128)(2,1)} %get-tuple-element.241.w1, f32[1,1408]{1,0:T(1,128)} %get-tuple-element.293.w1e, ...), custom_call_target="tpu_custom_call", output_to_operand_aliasing={{0}: (8, {}), {1}: (9, {}), {2}: (10, {})} | custom-call | flops 16928000000 | bytes 1000 | tf_op jit(solution)/shard_map/mlp/pallas_call | solution.py:617
  713.6 16.1 %mlp_back.7 = (f32[2208,1408]{1,0:T(8,128)}, f32[2208,641]{1,0:T(8,128)}, f32[1,1408]{1,0:T(1,128)}, f32[1,640]{1,0:T(1,128)}) custom-call(f32[736,640]{1,0:T(8,128)} %constant_dynamic-update-slice_fusion.16.g_ref, f32[2208,1408]{1,0:T(8,128)} %get-tuple-element.290.slope_ref, ...), custom_call_target="tpu_custom_call", output_to_operand_aliasing={{0}: (5, {}), {1}: (6, {})} | custom-call | flops 15456000000 | bytes 1000 | tf_op jit(solution)/shard_map/mlp_back/pallas_call | solution.py:669
  743.9 8.8 crps.5
  756.9 6.9 collective-permute-done.34
  765.8 8.6 collective-permute-done.24
  774.4 9.3 collective-permute-done.25
  785.6 16.8 %mlp_back.8 = (f32[2208,1408]{1,0:T(8,128)}, f32[2208,641]{1,0:T(8,128)}, f32[1,1408]{1,0:T(1,128)}, f32[1,640]{1,0:T(1,128)}) custom-call(f32[736,640]{1,0:T(8,128)} %copy-done.11, f32[2208,1408]{1,0:T(8,128)} %get-tuple-element.359.slope_ref, bf16[3,640,1408]{2,1,0:T(8,128)(2,1)} %get-tuple-element.291.w2, bf16[3,1408,640]{2,1,0:T(8,128)(2,1)} %get-tuple-element.292.w1, ...), custom_call_target="tpu_custom_call" | custom-call | flops 15456000000 | bytes 1000 | tf_op jit(solution)/shard_map/mlp_back/pallas_call | solution.py:669
  805.9 16.1 %mlp_back.9 = (f32[2208,1408]{1,0:T(8,128)}, f32[2208,641]{1,0:T(8,128)}, f32[1,1408]{1,0:T(1,128)}, f32[1,640]{1,0:T(1,128)}) custom-call(f32[736,640]{1,0:T(8,128)} %copy-done.13, f32[2208,1408]{1,0:T(8,128)} %get-tuple-element.290.slope_ref, bf16[3,640,1408]{2,1,0:T(8,128)(2,1)} %get-tuple-element.291.w2, ...), custom_call_target="tpu_custom_call", output_to_operand_aliasing={{0}: (5, {}), {1}: (6, {})} | custom-call | flops 15456000000 | bytes 1000 | tf_op jit(solution)/shard_map/mlp_back/pallas_call | solution.py:669
  849.4 16.1 %mlp_back.10 = (f32[2208,1408]{1,0:T(8,128)}, f32[2208,641]{1,0:T(8,128)}, f32[1,1408]{1,0:T(1,128)}, f32[1,640]{1,0:T(1,128)}) custom-call(f32[736,640]{1,0:T(8,128)} %constant_dynamic-update-slice_fusion.8.g_ref, f32[2208,1408]{1,0:T(8,128)} %get-tuple-element.359.slope_ref, ...), custom_call_target="tpu_custom_call", output_to_operand_aliasing={{0}: (5, {}), {1}: (6, {})} | custom-call | flops 15456000000 | bytes 1000 | tf_op jit(solution)/shard_map/mlp_back/pallas_call | solution.py:669
  865.5 16.1 %mlp_back.11 = (f32[2208,1408]{1,0:T(8,128)}, f32[2208,641]{1,0:T(8,128)}, f32[1,1408]{1,0:T(1,128)}, f32[1,640]{1,0:T(1,128)}) custom-call(f32[736,640]{1,0:T(8,128)} %constant_dynamic-update-slice_fusion.12.g_ref, f32[2208,1408]{1,0:T(8,128)} %get-tuple-element.359.slope_ref, ...), custom_call_target="tpu_custom_call", output_to_operand_aliasing={{0}: (5, {}), {1}: (6, {})} | custom-call | flops 15456000000 | bytes 1000 | tf_op jit(solution)/shard_map/mlp_back/pallas_call | solution.py:669
  887.8 12.4 analysis.11
  905.2 8.1 fusion.8
  913.4 7.6 fusion.6
  926.9 7.1 fusion.2
  934.0 7.2 fusion
  941.2 11.9 add_add_fusion
  953.1 19.3 %fusion.55 = f32[641,1408]{1,0:T(8,128)S(1)} fusion(f32[2208,641]{1,0:T(8,128)} %bitcast.148, f32[2208,1408]{1,0:T(8,128)} %get-tuple-element.390), kind=kOutput, calls=%fused_computation.162 | convolution fusion | flops 11956690944 | bytes 21706880 | tf_op jit(solution)/shard_map/tc,th->ch/dot_general | solution.py:1057
  972.5 22.8 %convolution_add_fusion = f32[641,1408]{1,0:T(8,128)} fusion(f32[641,1408]{1,0:T(8,128)S(1)} %fusion.55, f32[2208,641]{1,0:T(8,128)S(1)} %bitcast.114, f32[2208,1408]{1,0:T(8,128)} %get-tuple-element.391), kind=kOutput, calls=%fused_computation.22 | convolution fusion | flops 11957594112 | bytes 25316992 | tf_op jit(solution)/shard_map/tc,th->ch/dot_general | solution.py:1057
  995.3 12.0 filter_back.3
  1007.3 28.2 %all-to-all-done.9 = f32[8,12,24,640]{3,2,1,0:T(8,128)} async-done(((f32[8,12,24,640]{3,2,1,0:T(8,128)}), f32[8,12,24,640]{3,2,1,0:T(8,128)}, u32[]{:S(2)}, u32[]{:S(2)}) %all-to-all-start.9) | async-done | bytes 5898272 | tf_op jit(solution)/shard_map/all_to_all | solution.py:879
  1052.2 12.0 filter_back.2
  1072.5 133.3 %scatter_sum.1 = (f32[96,1408]{1,0:T(8,128)}, f32[96,1408]{1,0:T(8,128)}) custom-call(f32[768,1408]{1,0:T(8,128)} %select_maximum_fusion.refs_0_, f32[768,1408]{1,0:T(8,128)} %pad.48.refs_1_), custom_call_target="tpu_custom_call" | custom-call | flops 80000000000 | bytes 1000 | tf_op jit(solution)/shard_map/scatter_sum/pallas_call | solution.py:391
  1210.6 46.1 %gather.1 = (f32[768,1408]{1,0:T(8,128)}, f32[768,1408]{1,0:T(8,128)}) custom-call(f32[96,1408]{1,0:T(8,128)} %get-tuple-element.424.refs_0_, f32[96,1408]{1,0:T(8,128)} %get-tuple-element.425.refs_1_), custom_call_target="tpu_custom_call" | custom-call | flops 40000000000 | bytes 1000 | tf_op jit(solution)/shard_map/gather/pallas_call | solution.py:413
  1272.8 11.0 maximum_multiply_fusion
  1283.8 19.7 %copy.93 = f32[2,12,180,641]{3,0,2,1:T(2,128)} copy(f32[2,12,180,641]{3,2,1,0:T(8,128)} %maximum_multiply_fusion) | data formatting | bytes 22152960
  1314.7 13.0 synthesis.10.refs_0_
  1327.7 13.4 all-to-all-done.11.y_ref
  1341.1 16.5 %synthesis.11 = f32[12,180,2,633]{3,2,1,0:T(2,128)} custom-call(f32[8,12,24,640]{3,2,1,0:T(8,128)} %all-to-all-done.11.y_ref, bf16[184,192]{1,0:T(8,128)(2,1)} %constant.102.clone.th_ref, bf16[184,192]{1,0:T(8,128)(2,1)} %constant.103.clone.tl_ref, f32[12,184,641]{2,1,0:T(8,128)} %bitcast.137, f32[12,184,641]{2,1,0:T(8,128)} %synthesis.10.refs_0_), custom_call_target="tpu_custom_call" | custom-call | flops 14400000000 | bytes 1000 | tf_op jit(solution)/shard_map/synthesis/pallas_call | solution.py:250
  (340 shorter events, 281.3 us)
Async XLA Ops:
  21.7 137.0 %all-to-all-start = ((f32[8,12,24,640]{3,2,1,0:T(8,128)}), f32[8,12,24,640]{3,2,1,0:T(8,128)}, u32[]{:S(2)}, u32[]{:S(2)}) async-start(f32[8,12,24,640]{3,2,1,0:T(8,128)} %get-tuple-element.222), calls=%async_computation | async-start | bytes 11796480 | tf_op jit(solution)/shard_map/all_to_all | solution.py:879
  158.6 135.4 %all-to-all-start.1 = ((f32[8,12,24,640]{3,2,1,0:T(8,128)}), f32[8,12,24,640]{3,2,1,0:T(8,128)}, u32[]{:S(2)}, u32[]{:S(2)}) async-start(f32[8,12,24,640]{3,2,1,0:T(8,128)} %get-tuple-element.227), calls=%async_computation.1 | async-start | bytes 11796480 | tf_op jit(solution)/shard_map/all_to_all | solution.py:879
  294.0 135.5 %all-to-all-start.2 = ((f32[8,12,24,640]{3,2,1,0:T(8,128)}), f32[8,12,24,640]{3,2,1,0:T(8,128)}, u32[]{:S(2)}, u32[]{:S(2)}) async-start(f32[8,12,24,640]{3,2,1,0:T(8,128)} %bitcast.119), calls=%async_computation.2 | async-start | bytes 11796480 | tf_op jit(solution)/shard_map/all_to_all | solution.py:879
  429.5 57.1 %all-to-all-start.3 = ((f32[8,4,24,640]{3,2,1,0:T(8,128)}), f32[8,4,24,640]{3,2,1,0:T(8,128)S(1)}, u32[]{:S(2)}, u32[]{:S(2)}) async-start(f32[8,4,24,640]{3,2,1,0:T(8,128)} %bitcast.129), calls=%async_computation.3 | async-start | bytes 3932160 | tf_op jit(solution)/shard_map/all_to_all | solution.py:879
  465.9 55.1 %collective-permute-start = (f32[184,640]{1,0:T(8,128)S(1)}, f32[184,640]{1,0:T(8,128)}, u32[]{:S(2)}, u32[]{:S(2)}) collective-permute-start(f32[184,640]{1,0:T(8,128)S(1)} %get-tuple-element.473), channel_id=1, source_target_pairs={{0,8},{8,0},{16,24},{24,16},{1,9},{9,1},{17,25},{25,17},{2,10},{10... | collective-permute-start | bytes 1413128 | tf_op jit(solution)/shard_map/ppermute | solution.py:886
  467.3 71.3 %collective-permute-start.2 = (f32[184,640]{1,0:T(8,128)S(1)}, f32[184,640]{1,0:T(8,128)}, u32[]{:S(2)}, u32[]{:S(2)}) collective-permute-start(f32[184,640]{1,0:T(8,128)S(1)} %get-tuple-element.472), channel_id=1, source_target_pairs={{0,16},{8,24},{16,0},{24,8},{1,17},{9,25},{17,1},{25,9},{2,18},{10... | collective-permute-start | bytes 1413128 | tf_op jit(solution)/shard_map/ppermute | solution.py:886
  468.8 69.8 %collective-permute-start.4 = (f32[184,640]{1,0:T(8,128)S(1)}, f32[184,640]{1,0:T(8,128)}, u32[]{:S(2)}, u32[]{:S(2)}) collective-permute-start(f32[184,640]{1,0:T(8,128)S(1)} %get-tuple-element.471), channel_id=1, source_target_pairs={{0,24},{8,16},{16,8},{24,0},{1,25},{9,17},{17,9},{25,1},{2,26},{10... | collective-permute-start | bytes 1413128 | tf_op jit(solution)/shard_map/ppermute | solution.py:886
  492.9 94.6 %all-to-all-start.4 = ((f32[8,4,24,640]{3,2,1,0:T(8,128)}), f32[8,4,24,640]{3,2,1,0:T(8,128)S(1)}, u32[]{:S(2)}, u32[]{:S(2)}) async-start(f32[8,4,24,640]{3,2,1,0:T(8,128)} %bitcast.127), calls=%async_computation.4 | async-start | bytes 3932160 | tf_op jit(solution)/shard_map/all_to_all | solution.py:879
  518.0 20.7 %collective-permute-start.1 = (f32[184,640]{1,0:T(8,128)S(1)}, f32[184,640]{1,0:T(8,128)S(1)}, u32[]{:S(2)}, u32[]{:S(2)}) collective-permute-start(f32[184,640]{1,0:T(8,128)S(1)} %get-tuple-element.469), channel_id=1, source_target_pairs={{0,8},{8,0},{16,24},{24,16},{1,9},{9,1},{17,25},{25,17},{2,10},{10... | collective-permute-start | bytes 1413128 | tf_op jit(solution)/shard_map/ppermute | solution.py:886
  519.5 23.0 %collective-permute-start.3 = (f32[184,640]{1,0:T(8,128)S(1)}, f32[184,640]{1,0:T(8,128)S(1)}, u32[]{:S(2)}, u32[]{:S(2)}) collective-permute-start(f32[184,640]{1,0:T(8,128)S(1)} %get-tuple-element.468), channel_id=1, source_target_pairs={{0,16},{8,24},{16,0},{24,8},{1,17},{9,25},{17,1},{25,9},{2,18},{10... | collective-permute-start | bytes 1413128 | tf_op jit(solution)/shard_map/ppermute | solution.py:886
  521.0 21.5 %collective-permute-start.5 = (f32[184,640]{1,0:T(8,128)S(1)}, f32[184,640]{1,0:T(8,128)S(1)}, u32[]{:S(2)}, u32[]{:S(2)}) collective-permute-start(f32[184,640]{1,0:T(8,128)S(1)} %get-tuple-element.467), channel_id=1, source_target_pairs={{0,24},{8,16},{16,8},{24,0},{1,25},{9,17},{17,9},{25,1},{2,26},{10... | collective-permute-start | bytes 1413128 | tf_op jit(solution)/shard_map/ppermute | solution.py:886
  552.2 14.0 %collective-permute-start.12 = (f32[184,640]{1,0:T(8,128)}, f32[184,640]{1,0:T(8,128)S(1)}, u32[]{:S(2)}, u32[]{:S(2)}) collective-permute-start(f32[184,640]{1,0:T(8,128)} %get-tuple-element.286), channel_id=1, source_target_pairs={{0,8},{8,0},{16,24},{24,16},{1,9},{9,1},{17,25},{25,17},{2,10},{10... | collective-permute-start | bytes 1413128 | tf_op jit(solution)/shard_map/ppermute | solution.py:886
  553.4 32.5 %collective-permute-start.13 = (f32[184,640]{1,0:T(8,128)}, f32[184,640]{1,0:T(8,128)S(1)}, u32[]{:S(2)}, u32[]{:S(2)}) collective-permute-start(f32[184,640]{1,0:T(8,128)} %get-tuple-element.287), channel_id=1, source_target_pairs={{0,16},{8,24},{16,0},{24,8},{1,17},{9,25},{17,1},{25,9},{2,18},{10... | collective-permute-start | bytes 1413128 | tf_op jit(solution)/shard_map/ppermute | solution.py:886
  554.6 32.2 %collective-permute-start.14 = (f32[184,640]{1,0:T(8,128)}, f32[184,640]{1,0:T(8,128)S(1)}, u32[]{:S(2)}, u32[]{:S(2)}) collective-permute-start(f32[184,640]{1,0:T(8,128)} %get-tuple-element.288), channel_id=1, source_target_pairs={{0,24},{8,16},{16,8},{24,0},{1,25},{9,17},{17,9},{25,1},{2,26},{10... | collective-permute-start | bytes 1413128 | tf_op jit(solution)/shard_map/ppermute | solution.py:886
  556.6 64.4 %collective-permute-start.10 = (f32[184,640]{1,0:T(8,128)S(1)}, f32[184,640]{1,0:T(8,128)}, u32[]{:S(2)}, u32[]{:S(2)}) collective-permute-start(f32[184,640]{1,0:T(8,128)S(1)} %get-tuple-element.463), channel_id=1, source_target_pairs={{0,24},{8,16},{16,8},{24,0},{1,25},{9,17},{17,9},{25,1},{2,26},{10... | collective-permute-start | bytes 1413128 | tf_op jit(solution)/shard_map/ppermute | solution.py:886
  558.5 84.2 %collective-permute-start.6 = (f32[184,640]{1,0:T(8,128)S(1)}, f32[184,640]{1,0:T(8,128)}, u32[]{:S(2)}, u32[]{:S(2)}) collective-permute-start(f32[184,640]{1,0:T(8,128)S(1)} %get-tuple-element.465), channel_id=1, source_target_pairs={{0,8},{8,0},{16,24},{24,16},{1,9},{9,1},{17,25},{25,17},{2,10},{10... | collective-permute-start | bytes 1413128 | tf_op jit(solution)/shard_map/ppermute | solution.py:886
  566.2 76.5 %collective-permute-start.8 = (f32[184,640]{1,0:T(8,128)S(1)}, f32[184,640]{1,0:T(8,128)}, u32[]{:S(2)}, u32[]{:S(2)}) collective-permute-start(f32[184,640]{1,0:T(8,128)S(1)} %get-tuple-element.464), channel_id=1, source_target_pairs={{0,16},{8,24},{16,0},{24,8},{1,17},{9,25},{17,1},{25,9},{2,18},{10... | collective-permute-start | bytes 1413128 | tf_op jit(solution)/shard_map/ppermute | solution.py:886
  611.2 68.7 %all-to-all-start.5 = ((f32[8,4,24,640]{3,2,1,0:T(8,128)}), f32[8,4,24,640]{3,2,1,0:T(8,128)S(1)}, u32[]{:S(2)}, u32[]{:S(2)}) async-start(f32[8,4,24,640]{3,2,1,0:T(8,128)} %bitcast.125), calls=%async_computation.5 | async-start | bytes 3932160 | tf_op jit(solution)/shard_map/all_to_all | solution.py:879
  618.3 24.3 %collective-permute-start.11 = (f32[184,640]{1,0:T(8,128)S(1)}, f32[184,640]{1,0:T(8,128)S(1)}, u32[]{:S(2)}, u32[]{:S(2)}) collective-permute-start(f32[184,640]{1,0:T(8,128)S(1)} %get-tuple-element.459), channel_id=1, source_target_pairs={{0,24},{8,16},{16,8},{24,0},{1,25},{9,17},{17,9},{25,1},{2,26},{10... | collective-permute-start | bytes 1413128 | tf_op jit(solution)/shard_map/ppermute | solution.py:886
  621.0 21.6 %collective-permute-start.7 = (f32[184,640]{1,0:T(8,128)S(1)}, f32[184,640]{1,0:T(8,128)S(1)}, u32[]{:S(2)}, u32[]{:S(2)}) collective-permute-start(f32[184,640]{1,0:T(8,128)S(1)} %get-tuple-element.461), channel_id=1, source_target_pairs={{0,8},{8,0},{16,24},{24,16},{1,9},{9,1},{17,25},{25,17},{2,10},{10... | collective-permute-start | bytes 1413128 | tf_op jit(solution)/shard_map/ppermute | solution.py:886
  621.0 21.6 %collective-permute-start.9 = (f32[184,640]{1,0:T(8,128)S(1)}, f32[184,640]{1,0:T(8,128)S(1)}, u32[]{:S(2)}, u32[]{:S(2)}) collective-permute-start(f32[184,640]{1,0:T(8,128)S(1)} %get-tuple-element.460), channel_id=1, source_target_pairs={{0,16},{8,24},{16,0},{24,8},{1,17},{9,25},{17,1},{25,9},{2,18},{10... | collective-permute-start | bytes 1413128 | tf_op jit(solution)/shard_map/ppermute | solution.py:886
  652.5 14.0 %collective-permute-start.21 = (f32[184,640]{1,0:T(8,128)}, f32[184,640]{1,0:T(8,128)S(1)}, u32[]{:S(2)}, u32[]{:S(2)}) collective-permute-start(f32[184,640]{1,0:T(8,128)} %get-tuple-element.312), channel_id=1, source_target_pairs={{0,8},{8,0},{16,24},{24,16},{1,9},{9,1},{17,25},{25,17},{2,10},{10... | collective-permute-start | bytes 1413128 | tf_op jit(solution)/shard_map/ppermute | solution.py:886
  654.3 24.0 %collective-permute-start.22 = (f32[184,640]{1,0:T(8,128)}, f32[184,640]{1,0:T(8,128)S(1)}, u32[]{:S(2)}, u32[]{:S(2)}) collective-permute-start(f32[184,640]{1,0:T(8,128)} %get-tuple-element.313), channel_id=1, source_target_pairs={{0,16},{8,24},{16,0},{24,8},{1,17},{9,25},{17,1},{25,9},{2,18},{10... | collective-permute-start | bytes 1413128 | tf_op jit(solution)/shard_map/ppermute | solution.py:886
  656.2 22.9 %collective-permute-start.23 = (f32[184,640]{1,0:T(8,128)}, f32[184,640]{1,0:T(8,128)S(1)}, u32[]{:S(2)}, u32[]{:S(2)}) collective-permute-start(f32[184,640]{1,0:T(8,128)} %get-tuple-element.314), channel_id=1, source_target_pairs={{0,24},{8,16},{16,8},{24,0},{1,25},{9,17},{17,9},{25,1},{2,26},{10... | collective-permute-start | bytes 1413128 | tf_op jit(solution)/shard_map/ppermute | solution.py:886
  657.1 55.1 %collective-permute-start.15 = (f32[184,640]{1,0:T(8,128)S(1)}, f32[184,640]{1,0:T(8,128)}, u32[]{:S(2)}, u32[]{:S(2)}) collective-permute-start(f32[184,640]{1,0:T(8,128)S(1)} %get-tuple-element.457), channel_id=1, source_target_pairs={{0,8},{8,0},{16,24},{24,16},{1,9},{9,1},{17,25},{25,17},{2,10},{10... | collective-permute-start | bytes 1413128 | tf_op jit(solution)/shard_map/ppermute | solution.py:886
  658.7 81.6 %collective-permute-start.17 = (f32[184,640]{1,0:T(8,128)S(1)}, f32[184,640]{1,0:T(8,128)}, u32[]{:S(2)}, u32[]{:S(2)}) collective-permute-start(f32[184,640]{1,0:T(8,128)S(1)} %get-tuple-element.456), channel_id=1, source_target_pairs={{0,16},{8,24},{16,0},{24,8},{1,17},{9,25},{17,1},{25,9},{2,18},{10... | collective-permute-start | bytes 1413128 | tf_op jit(solution)/shard_map/ppermute | solution.py:886
  666.5 74.5 %collective-permute-start.19 = (f32[184,640]{1,0:T(8,128)S(1)}, f32[184,640]{1,0:T(8,128)}, u32[]{:S(2)}, u32[]{:S(2)}) collective-permute-start(f32[184,640]{1,0:T(8,128)S(1)} %get-tuple-element.455), channel_id=1, source_target_pairs={{0,24},{8,16},{16,8},{24,0},{1,25},{9,17},{17,9},{25,1},{2,26},{10... | collective-permute-start | bytes 1413128 | tf_op jit(solution)/shard_map/ppermute | solution.py:886
  679.9 51.6 %all-to-all-start.6 = ((f32[8,4,24,640]{3,2,1,0:T(8,128)}), f32[8,4,24,640]{3,2,1,0:T(8,128)}, u32[]{:S(2)}, u32[]{:S(2)}) async-start(f32[8,4,24,640]{3,2,1,0:T(8,128)} %analysis.8), calls=%async_computation.6 | async-start | bytes 3932160 | tf_op jit(solution)/shard_map/all_to_all | solution.py:879
  710.1 32.4 %collective-permute-start.16 = (f32[184,640]{1,0:T(8,128)}, f32[184,640]{1,0:T(8,128)}, u32[]{:S(2)}, u32[]{:S(2)}) collective-permute-start(f32[184,640]{1,0:T(8,128)} %get-tuple-element.453), channel_id=1, source_target_pairs={{0,8},{8,0},{16,24},{24,16},{1,9},{9,1},{17,25},{25,17},{2,10},{10... | collective-permute-start | bytes 1413128 | tf_op jit(solution)/shard_map/ppermute | solution.py:886
  710.8 33.1 %collective-permute-start.18 = (f32[184,640]{1,0:T(8,128)}, f32[184,640]{1,0:T(8,128)}, u32[]{:S(2)}, u32[]{:S(2)}) collective-permute-start(f32[184,640]{1,0:T(8,128)} %get-tuple-element.452), channel_id=1, source_target_pairs={{0,16},{8,24},{16,0},{24,8},{1,17},{9,25},{17,1},{25,9},{2,18},{10... | collective-permute-start | bytes 1413128 | tf_op jit(solution)/shard_map/ppermute | solution.py:886
  712.2 31.7 %collective-permute-start.20 = (f32[184,640]{1,0:T(8,128)S(1)}, f32[184,640]{1,0:T(8,128)}, u32[]{:S(2)}, u32[]{:S(2)}) collective-permute-start(f32[184,640]{1,0:T(8,128)S(1)} %get-tuple-element.451), channel_id=1, source_target_pairs={{0,24},{8,16},{16,8},{24,0},{1,25},{9,17},{17,9},{25,1},{2,26},{10... | collective-permute-start | bytes 1413128 | tf_op jit(solution)/shard_map/ppermute | solution.py:886
  736.3 95.0 %all-to-all-start.7 = ((f32[8,4,24,640]{3,2,1,0:T(8,128)}), f32[8,4,24,640]{3,2,1,0:T(8,128)S(1)}, u32[]{:S(2)}, u32[]{:S(2)}) async-start(f32[8,4,24,640]{3,2,1,0:T(8,128)} %analysis.9), calls=%async_computation.7 | async-start | bytes 3932160 | tf_op jit(solution)/shard_map/all_to_all | solution.py:879
  740.3 15.2 %collective-permute-start.33 = (f32[184,640]{1,0:T(8,128)}, f32[184,640]{1,0:T(8,128)S(1)}, u32[]{:S(2)}, u32[]{:S(2)}) collective-permute-start(f32[184,640]{1,0:T(8,128)} %get-tuple-element.355), channel_id=1, source_target_pairs={{0,8},{8,0},{16,24},{24,16},{1,9},{9,1},{17,25},{25,17},{2,10},{10... | collective-permute-start | bytes 1413128 | tf_op jit(solution)/shard_map/ppermute | solution.py:886
  741.1 22.8 %collective-permute-start.34 = (f32[184,640]{1,0:T(8,128)}, f32[184,640]{1,0:T(8,128)S(1)}, u32[]{:S(2)}, u32[]{:S(2)}) collective-permute-start(f32[184,640]{1,0:T(8,128)} %get-tuple-element.356), channel_id=1, source_target_pairs={{0,16},{8,24},{16,0},{24,8},{1,17},{9,25},{17,1},{25,9},{2,18},{10... | collective-permute-start | bytes 1413128 | tf_op jit(solution)/shard_map/ppermute | solution.py:886
  742.5 23.3 %collective-permute-start.35 = (f32[184,640]{1,0:T(8,128)}, f32[184,640]{1,0:T(8,128)S(1)}, u32[]{:S(2)}, u32[]{:S(2)}) collective-permute-start(f32[184,640]{1,0:T(8,128)} %get-tuple-element.357), channel_id=1, source_target_pairs={{0,24},{8,16},{16,8},{24,0},{1,25},{9,17},{17,9},{25,1},{2,26},{10... | collective-permute-start | bytes 1413128 | tf_op jit(solution)/shard_map/ppermute | solution.py:886
  752.7 21.7 %collective-permute-start.24 = (f32[184,640]{1,0:T(8,128)}, f32[184,640]{1,0:T(8,128)S(1)}, u32[]{:S(2)}, u32[]{:S(2)}) collective-permute-start(f32[184,640]{1,0:T(8,128)} %get-tuple-element.332), channel_id=1, source_target_pairs={{0,8},{8,0},{16,24},{24,16},{1,9},{9,1},{17,25},{25,17},{2,10},{10... | collective-permute-start | bytes 1413128 | tf_op jit(solution)/shard_map/ppermute | solution.py:886
  753.5 30.2 %collective-permute-start.25 = (f32[184,640]{1,0:T(8,128)}, f32[184,640]{1,0:T(8,128)S(1)}, u32[]{:S(2)}, u32[]{:S(2)}) collective-permute-start(f32[184,640]{1,0:T(8,128)} %get-tuple-element.334), channel_id=1, source_target_pairs={{0,16},{8,24},{16,0},{24,8},{1,17},{9,25},{17,1},{25,9},{2,18},{10... | collective-permute-start | bytes 1413128 | tf_op jit(solution)/shard_map/ppermute | solution.py:886
  755.5 29.9 %collective-permute-start.26 = (f32[184,640]{1,0:T(8,128)S(1)}, f32[184,640]{1,0:T(8,128)S(1)}, u32[]{:S(2)}, u32[]{:S(2)}) collective-permute-start(f32[184,640]{1,0:T(8,128)S(1)} %copy-done.50), channel_id=1, source_target_pairs={{0,24},{8,16},{16,8},{24,0},{1,25},{9,17},{17,9},{25,1},{2,26},{10... | collective-permute-start | bytes 1413128 | tf_op jit(solution)/shard_map/ppermute | solution.py:886
  802.4 21.9 %collective-permute-start.27 = (f32[184,640]{1,0:T(8,128)S(1)}, f32[184,640]{1,0:T(8,128)S(1)}, u32[]{:S(2)}, u32[]{:S(2)}) collective-permute-start(f32[184,640]{1,0:T(8,128)S(1)} %copy-done.49), channel_id=1, source_target_pairs={{0,8},{8,0},{16,24},{24,16},{1,9},{9,1},{17,25},{25,17},{2,10},{10... | collective-permute-start | bytes 1413128 | tf_op jit(solution)/shard_map/ppermute | solution.py:886
  803.0 22.5 %collective-permute-start.28 = (f32[184,640]{1,0:T(8,128)S(1)}, f32[184,640]{1,0:T(8,128)S(1)}, u32[]{:S(2)}, u32[]{:S(2)}) collective-permute-start(f32[184,640]{1,0:T(8,128)S(1)} %copy-done.48), channel_id=1, source_target_pairs={{0,16},{8,24},{16,0},{24,8},{1,17},{9,25},{17,1},{25,9},{2,18},{10... | collective-permute-start | bytes 1413128 | tf_op jit(solution)/shard_map/ppermute | solution.py:886
  804.8 20.8 %collective-permute-start.29 = (f32[184,640]{1,0:T(8,128)S(1)}, f32[184,640]{1,0:T(8,128)S(1)}, u32[]{:S(2)}, u32[]{:S(2)}) collective-permute-start(f32[184,640]{1,0:T(8,128)S(1)} %copy-done.47), channel_id=1, source_target_pairs={{0,24},{8,16},{16,8},{24,0},{1,25},{9,17},{17,9},{25,1},{2,26},{10... | collective-permute-start | bytes 1413128 | tf_op jit(solution)/shard_map/ppermute | solution.py:886
  825.5 17.7 %collective-permute-start.30 = (f32[184,640]{1,0:T(8,128)}, f32[184,640]{1,0:T(8,128)}, u32[]{:S(2)}, u32[]{:S(2)}) collective-permute-start(f32[184,640]{1,0:T(8,128)} %get-tuple-element.347), channel_id=1, source_target_pairs={{0,8},{8,0},{16,24},{24,16},{1,9},{9,1},{17,25},{25,17},{2,10},{10... | collective-permute-start | bytes 1413128 | tf_op jit(solution)/shard_map/ppermute | solution.py:886
  826.6 20.1 %collective-permute-start.31 = (f32[184,640]{1,0:T(8,128)}, f32[184,640]{1,0:T(8,128)}, u32[]{:S(2)}, u32[]{:S(2)}) collective-permute-start(f32[184,640]{1,0:T(8,128)} %get-tuple-element.348), channel_id=1, source_target_pairs={{0,16},{8,24},{16,0},{24,8},{1,17},{9,25},{17,1},{25,9},{2,18},{10... | collective-permute-start | bytes 1413128 | tf_op jit(solution)/shard_map/ppermute | solution.py:886
  827.3 21.3 %collective-permute-start.32 = (f32[184,640]{1,0:T(8,128)}, f32[184,640]{1,0:T(8,128)S(1)}, u32[]{:S(2)}, u32[]{:S(2)}) collective-permute-start(f32[184,640]{1,0:T(8,128)} %get-tuple-element.349), channel_id=1, source_target_pairs={{0,24},{8,16},{16,8},{24,0},{1,25},{9,17},{17,9},{25,1},{2,26},{10... | collective-permute-start | bytes 1413128 | tf_op jit(solution)/shard_map/ppermute | solution.py:886
  836.6 51.2 %all-to-all-start.8 = ((f32[8,4,24,640]{3,2,1,0:T(8,128)}), f32[8,4,24,640]{3,2,1,0:T(8,128)S(1)}, u32[]{:S(2)}, u32[]{:S(2)}) async-start(f32[8,4,24,640]{3,2,1,0:T(8,128)} %analysis.10), calls=%async_computation.8 | async-start | bytes 3932160 | tf_op jit(solution)/shard_map/all_to_all | solution.py:879
  900.2 135.3 %all-to-all-start.9 = ((f32[8,12,24,640]{3,2,1,0:T(8,128)}), f32[8,12,24,640]{3,2,1,0:T(8,128)}, u32[]{:S(2)}, u32[]{:S(2)}) async-start(f32[8,12,24,640]{3,2,1,0:T(8,128)} %analysis.11), calls=%async_computation.9 | async-start | bytes 11796480 | tf_op jit(solution)/shard_map/all_to_all | solution.py:879
  1035.6 170.2 %all-to-all-start.10 = ((f32[8,12,24,640]{3,2,1,0:T(8,128)}), f32[8,12,24,640]{3,2,1,0:T(8,128)}, u32[]{:S(2)}, u32[]{:S(2)}) async-start(f32[8,12,24,640]{3,2,1,0:T(8,128)} %bitcast.120), calls=%async_computation.10 | async-start | bytes 11796480 | tf_op jit(solution)/shard_map/all_to_all | solution.py:879
  1205.8 135.3 %all-to-all-start.11 = ((f32[8,12,24,640]{3,2,1,0:T(8,128)}), f32[8,12,24,640]{3,2,1,0:T(8,128)}, u32[]{:S(2)}, u32[]{:S(2)}) async-start(f32[8,12,24,640]{3,2,1,0:T(8,128)} %bitcast.121), calls=%async_computation.11 | async-start | bytes 11796480 | tf_op jit(solution)/shard_map/all_to_all | solution.py:879
  (67 other events, 559.4 us)
